TPU v7x, 512 devices: a whole 4x8x8 slice. The times are simulated.
512 devices in a mesh: ta: 16 (over y, core), gz: 8 (over z), gy: 4 (over x).
Axes of the slice: x: 4, y: 8, z: 8, core: 2. Of those that a mesh axis runs over, the one named last changes fastest.
Arguments:
- residual: bfloat16 [2, 4, 3, 16, 16, 8, 4, 512], P(None, None, None, None, 'ta', 'gz', 'gy'), may hold values from -40 to 40
- null_vectors: bfloat16 [2, 24, 4, 3, 16, 8, 4, 512], P(None, None, None, None, 'ta', 'gz', 'gy'), may hold values from -0.078125 to 0.078125
- coarse_op: bfloat16 [16, 8, 4, 9, 2, 48, 48], P(None, 'gz', 'gy'), may hold values from -1 to 1
Outputs:
- correction: bfloat16 [2, 4, 3, 16, 16, 8, 4, 512], P(None, None, None, None, 'ta', 'gz', 'gy')
- coarse_residual: float32 [2, 48, 16, 8, 4, 16], P(None, None, 'ta', 'gz', 'gy')
All inputs are finite; a program needn't handle non-finite values.
Results may differ from a plain program's by a relative error of at most 0.009.
Values may be sent and summed in bfloat16 or wider, within the bound.
A program may use at most 64 MiB of HBM per device.

v0:
```python
import jax
import jax.numpy as jnp
from jax import lax
from jax.sharding import PartitionSpec as P

ITERS = 4


HIGH = lax.Precision.HIGHEST


def extended(cells, sides, width):
    for axis, dim in sides:
        count = lax.axis_size(axis)
        head = lax.slice_in_dim(cells, 0, width, axis=dim)
        tail = lax.slice_in_dim(cells, cells.shape[dim] - width, cells.shape[dim], axis=dim)
        cells = jnp.concatenate(
            [
                lax.ppermute(tail, axis, [(i, (i + 1) % count) for i in range(count)]),
                cells,
                lax.ppermute(head, axis, [((i + 1) % count, i) for i in range(count)]),
            ],
            axis=dim,
        )
    return cells


def restrict_local(null_vectors, residual):
    nvec = null_vectors.shape[1]
    sites = null_vectors.shape[-1]
    rhs = residual.shape[3]
    basis = null_vectors.reshape(2, nvec, 2, 2, 3, sites)
    source = residual.reshape(2, 2, 2, 3, rhs, sites)
    prod = jnp.einsum("pkcabs,qcabrs->pqckr", basis, source, preferred_element_type=jnp.float32)
    real = (prod[0, 0] + prod[1, 1]).reshape(2 * nvec, rhs)
    imag = (prod[0, 1] - prod[1, 0]).reshape(2 * nvec, rhs)
    return jnp.stack([real, imag]).reshape(2, 2 * nvec, 1, 1, 1, rhs)


def prolong_local(null_vectors, coarse):
    nvec = null_vectors.shape[1]
    sites = null_vectors.shape[-1]
    rhs = coarse.shape[-1]
    basis = null_vectors.reshape(2, nvec, 2, 2, 3, sites)
    values = coarse.reshape(2, 2, nvec, rhs)
    prod = jnp.einsum("pkcabs,qckr->pqcabrs", basis, values, preferred_element_type=jnp.float32)
    real = (prod[0, 0] - prod[1, 1]).reshape(4, 3, rhs, sites)
    imag = (prod[0, 1] + prod[1, 0]).reshape(4, 3, rhs, sites)
    return jnp.stack([real, imag]).astype(jnp.bfloat16).reshape(2, 4, 3, rhs, 1, 1, 1, sites)


def contract(left, right):
    return jnp.einsum("tzymij,mjtzyr->itzyr", left, right, precision=HIGH)


def apply_links(links, stacked):
    lreal = links[:, :, :, :, 0]
    limag = links[:, :, :, :, 1]
    real = contract(lreal, stacked[:, 0]) - contract(limag, stacked[:, 1])
    imag = contract(lreal, stacked[:, 1]) + contract(limag, stacked[:, 0])
    return jnp.stack([real, imag])


def neighbours(field):
    padded = extended(field.astype(jnp.bfloat16), (("gz", 3), ("gy", 4)), 1).astype(field.dtype)
    return jnp.stack(
        [
            field,
            jnp.roll(field, -1, 2),
            jnp.roll(field, 1, 2),
            padded[:, :, :, 2:3, 1:2],
            padded[:, :, :, 0:1, 1:2],
            padded[:, :, :, 1:2, 2:3],
            padded[:, :, :, 1:2, 0:1],
            field,
            field,
        ]
    )


def projections(values):
    return lax.psum(values, ("gz", "gy"))


def lengths(values):
    return lax.psum(values, ("gz", "gy"))


def inner(left, right):
    real = jnp.sum(left[0] * right[0] + left[1] * right[1], axis=(0, 1, 2, 3))
    imag = jnp.sum(left[0] * right[1] - left[1] * right[0], axis=(0, 1, 2, 3))
    return (real, imag)


def cscale(sreal, simag, field):
    return jnp.stack([sreal * field[0] - simag * field[1], sreal * field[1] + simag * field[0]])


def body(residual, null_vectors, coarse_op):
    right = restrict_local(null_vectors, residual)
    right = lax.all_gather(right, "ta", axis=2, tiled=True)
    links = coarse_op.astype(jnp.float32)
    solution = jnp.zeros_like(right)
    remain = right
    kept_q = []
    kept_p = []
    kept_n = []
    for step in range(ITERS):
        search = remain
        image = apply_links(links, neighbours(search))
        count = len(kept_q)
        if count > 0:
            pieces = []
            for prior in kept_q:
                pieces.extend(inner(prior, image))
            totals = projections(jnp.stack(pieces))
            for j in range(count):
                breal = totals[2 * j] / kept_n[j]
                bimag = totals[2 * j + 1] / kept_n[j]
                image = image - cscale(breal, bimag, kept_q[j])
                search = search - cscale(breal, bimag, kept_p[j])
        self_real = inner(image, image)[0]
        cross_real, cross_imag = inner(image, remain)
        sums = lengths(jnp.stack([self_real, cross_real, cross_imag]))
        square = sums[0]
        creal = sums[1]
        cimag = sums[2]
        areal = creal / square
        aimag = cimag / square
        solution = solution + cscale(areal, aimag, search)
        remain = remain - cscale(areal, aimag, image)
        kept_q.append(image)
        kept_p.append(search)
        kept_n.append(square)
    solution = lax.dynamic_slice_in_dim(solution, lax.axis_index("ta"), 1, 2)
    remain = lax.dynamic_slice_in_dim(remain, lax.axis_index("ta"), 1, 2)
    rounded = solution.astype(jnp.bfloat16)
    correction = prolong_local(null_vectors, rounded)
    return (correction, remain)


def solution(mesh):
    return jax.shard_map(
        body,
        mesh=mesh,
        in_specs=(
            P(None, None, None, None, "ta", "gz", "gy", None),
            P(None, None, None, None, "ta", "gz", "gy", None),
            P(None, "gz", "gy", None, None, None, None),
        ),
        out_specs=(
            P(None, None, None, None, "ta", "gz", "gy", None),
            P(None, None, "ta", "gz", "gy", None),
        ),
        check_vma=False,
    )
```

profile of v0, /device:TPU:8, one launch (start us, length us, event | category | flops | bytes accessed | tf_op | source)
XLA Modules:
  0.0 696.6 jit_solution(5653111014708903469)
XLA Ops:
  0.6 1.9 reshape.1461
  2.6 1.9 convolution_bitcast_fusion.17
  4.7 20.6 %all-gather = f32[2,48,256]{1,2,0:T(8,128)S(1)} all-gather(f32[2,48,16]{1,2,0:T(8,128)S(1)} %pad_maximum_fusion.21), channel_id=2, replica_groups=mesh['ta'=16,'gz'=8,'gy'=4] {'ta'}, dimensions={2}, use_global_device_ids=true | all-gather | bytes 104448 | tf_op jit(solution)/shard_map/all_gather | solution.py:101
  25.4 7.2 %collective-permute-start.1 = (bf16[2,48,16,1,1,16]{1,5,2,0,4,3:T(8,128)(2,1)S(1)}, bf16[2,48,16,1,1,16]{1,5,2,0,4,3:T(8,128)(2,1)S(1)}, u32[]{:S(2)}, u32[]{:S(2)}) collective-permute-start(bf16[2,48,16,1,1,16]{1,5,2,0,4,3:T(8,128)(2,1)S(1)} %convert_element_type.36), channel_id=1, source_target_pairs={{4,0},{8,4},{12,8},{16,12},{20,16},{24,20},{28,24},{0,28},{5,1},{9... | collective-permute-start | bytes 147464 | tf_op jit(solution)/shard_map/ppermute | solution.py:21
  32.5 1.9 collective-permute-start
  35.9 2.6 slice_bitcast_fusion
  39.3 1.7 collective-permute-done
  41.9 4.7 collective-permute-start.3
  46.6 1.9 collective-permute-start.2
  49.3 1.7 fusion.40
  51.0 3.6 collective-permute-done.3
  54.7 5.3 collective-permute-done.2
  61.7 1.8 fusion.37
  68.4 2.9 convolution_bitcast_fusion.16
  71.3 2.9 convolution_bitcast_fusion.14
  74.3 3.0 fusion.9
  77.3 3.8 add_reduce_fusion.2
  81.1 70.7 %psum.49 = f32[3,16]{1,0:T(4,128)S(1)} all-reduce(f32[3,16]{1,0:T(4,128)S(1)} %pad_maximum_fusion.22), channel_id=1, replica_groups=mesh['ta'=16,'gz'=8,'gy'=4] {'gz','gy'}, use_global_device_ids=true, to_apply=%region_3.4 | all-reduce | flops 48 | bytes 384 | tf_op jit(solution)/shard_map/psum | solution.py:86
  154.0 1.9 collective-permute-start.5
  155.9 3.9 collective-permute-start.4
  160.8 3.1 collective-permute-done.4
  164.1 3.4 collective-permute-start.7
  167.5 2.7 collective-permute-start.6
  170.2 3.7 collective-permute-done.7
  173.8 4.6 collective-permute-done.6
  183.6 2.4 fusion.98
  186.1 69.6 %psum.50 = f32[2,16]{1,0:T(2,128)S(1)} all-reduce(f32[2,16]{1,0:T(2,128)S(1)} %pad_maximum_fusion.27), channel_id=1, replica_groups=mesh['ta'=16,'gz'=8,'gy'=4] {'gz','gy'}, use_global_device_ids=true, to_apply=%region_6.7 | all-reduce | flops 32 | bytes 256 | tf_op jit(solution)/shard_map/psum | solution.py:82
  259.7 71.8 %psum.51 = f32[3,16]{1,0:T(4,128)S(1)} all-reduce(f32[3,16]{1,0:T(4,128)S(1)} %pad_maximum_fusion.23), channel_id=1, replica_groups=mesh['ta'=16,'gz'=8,'gy'=4] {'gz','gy'}, use_global_device_ids=true, to_apply=%region_10.11 | all-reduce | flops 48 | bytes 384 | tf_op jit(solution)/shard_map/psum | solution.py:86
  333.7 1.9 collective-permute-start.9
  335.7 3.9 collective-permute-start.8
  340.7 3.1 collective-permute-done.8
  343.9 2.3 collective-permute-start.11
  346.2 3.5 collective-permute-start.10
  349.8 3.8 collective-permute-done.11
  353.5 3.6 collective-permute-done.10
  362.3 2.5 fusion.82
  364.8 70.6 %psum.52 = f32[4,16]{1,0:T(4,128)} all-reduce(f32[4,16]{1,0:T(4,128)S(1)} %pad_maximum_fusion.24), channel_id=1, replica_groups=mesh['ta'=16,'gz'=8,'gy'=4] {'gz','gy'}, use_global_device_ids=true, to_apply=%region_15.16 | all-reduce | flops 64 | bytes 512 | tf_op jit(solution)/shard_map/psum | solution.py:82
  441.7 71.9 %psum.53 = f32[3,16]{1,0:T(4,128)} all-reduce(f32[3,16]{1,0:T(4,128)} %pad_maximum_fusion.25), channel_id=1, replica_groups=mesh['ta'=16,'gz'=8,'gy'=4] {'gz','gy'}, use_global_device_ids=true, to_apply=%region_19.20 | all-reduce | flops 48 | bytes 384 | tf_op jit(solution)/shard_map/psum | solution.py:86
  516.6 1.9 collective-permute-start.13
  518.6 3.9 collective-permute-start.12
  523.5 3.1 collective-permute-done.12
  526.7 3.1 collective-permute-start.15
  529.8 3.0 collective-permute-start.14
  532.9 3.6 collective-permute-done.15
  536.4 4.5 collective-permute-done.14
  546.3 2.5 fusion.62
  548.8 69.6 %psum.54 = f32[6,16]{1,0:T(8,128)S(1)} all-reduce(f32[6,16]{1,0:T(8,128)S(1)} %stack.436), channel_id=1, replica_groups=mesh['ta'=16,'gz'=8,'gy'=4] {'gz','gy'}, use_global_device_ids=true, to_apply=%region_26.27 | all-reduce | flops 96 | bytes 768 | tf_op jit(solution)/shard_map/psum | solution.py:82
  621.1 71.6 %psum.55 = f32[3,16]{1,0:T(4,128)S(1)} all-reduce(f32[3,16]{1,0:T(4,128)S(1)} %pad_maximum_fusion.26), channel_id=1, replica_groups=mesh['ta'=16,'gz'=8,'gy'=4] {'gz','gy'}, use_global_device_ids=true, to_apply=%region_30.31 | all-reduce | flops 48 | bytes 384 | tf_op jit(solution)/shard_map/psum | solution.py:86
  (229 shorter events, 53.3 us)
Async XLA Ops:
  2.5 32.7 %copy-start.28 = (bf16[2,24,2,2,3,512]{5,3,2,4,1,0:T(2,128)(2,1)}, bf16[2,24,2,2,3,512]{5,3,2,4,1,0:T(2,128)(2,1)S(1)}, u32[]{:S(2)}) copy-start(bf16[2,24,2,2,3,512]{5,3,2,4,1,0:T(2,128)(2,1)S(1)} %reshape.1461) | copy-start | bytes 1769476
  25.3 13.3 %copy-start.3 = (f32[2,48,256]{1,2,0:T(8,128)}, f32[2,48,256]{1,2,0:T(8,128)S(1)}, u32[]{:S(2)}) copy-start(f32[2,48,256]{1,2,0:T(8,128)S(1)} %all-gather) | copy-start | bytes 294916
  25.3 15.7 %copy-start.22 = (bf16[2,48,16,1,1,16]{1,5,2,0,4,3:T(8,128)(2,1)}, bf16[2,48,16,1,1,16]{1,5,2,0,4,3:T(8,128)(2,1)S(1)}, u32[]{:S(2)}) copy-start(bf16[2,48,16,1,1,16]{1,5,2,0,4,3:T(8,128)(2,1)S(1)} %convert_element_type.36) | copy-start | bytes 147460
  25.4 14.0 %collective-permute-start.1 = (bf16[2,48,16,1,1,16]{1,5,2,0,4,3:T(8,128)(2,1)S(1)}, bf16[2,48,16,1,1,16]{1,5,2,0,4,3:T(8,128)(2,1)S(1)}, u32[]{:S(2)}, u32[]{:S(2)}) collective-permute-start(bf16[2,48,16,1,1,16]{1,5,2,0,4,3:T(8,128)(2,1)S(1)} %convert_element_type.36), channel_id=1, source_target_pairs={{4,0},{8,4},{12,8},{16,12},{20,16},{24,20},{28,24},{0,28},{5,1},{9... | collective-permute-start | bytes 147464 | tf_op jit(solution)/shard_map/ppermute | solution.py:21
  32.5 8.6 %collective-permute-start = (bf16[2,48,16,1,1,16]{1,5,2,0,4,3:T(8,128)(2,1)S(1)}, bf16[2,48,16,1,1,16]{1,5,2,0,4,3:T(8,128)(2,1)S(1)}, u32[]{:S(2)}, u32[]{:S(2)}) collective-permute-start(bf16[2,48,16,1,1,16]{1,5,2,0,4,3:T(8,128)(2,1)S(1)} %convert_element_type.36), channel_id=1, source_target_pairs={{0,4},{4,8},{8,12},{12,16},{16,20},{20,24},{24,28},{28,0},{1,5},{5... | collective-permute-start | bytes 147464 | tf_op jit(solution)/shard_map/ppermute | solution.py:19
  39.3 2.6 copy-start.24
  41.1 5.5 copy-start.26
  41.9 12.7 %collective-permute-start.3 = (bf16[2,48,16,3,1,16]{1,5,2,0,4,3:T(8,128)(2,1)}, bf16[2,48,16,3,1,16]{1,5,2,0,4,3:T(8,128)(2,1)}, u32[]{:S(2)}, u32[]{:S(2)}) collective-permute-start(bf16[2,48,16,3,1,16]{1,5,2,0,4,3:T(8,128)(2,1)} %pad_maximum_fusion), channel_id=1, source_target_pairs={{1,0},{2,1},{3,2},{0,3},{5,4},{6,5},{7,6},{4,7},{9,8},{10,9},{11,1... | collective-permute-start | bytes 442376 | tf_op jit(solution)/shard_map/ppermute | solution.py:21
  46.6 13.4 %collective-permute-start.2 = (bf16[2,48,16,3,1,16]{1,5,2,0,4,3:T(8,128)(2,1)}, bf16[2,48,16,3,1,16]{1,5,2,0,4,3:T(8,128)(2,1)}, u32[]{:S(2)}, u32[]{:S(2)}) collective-permute-start(bf16[2,48,16,3,1,16]{1,5,2,0,4,3:T(8,128)(2,1)} %pad_maximum_fusion), channel_id=1, source_target_pairs={{0,1},{1,2},{2,3},{3,0},{4,5},{5,6},{6,7},{7,4},{8,9},{9,10},{10,1... | collective-permute-start | bytes 442376 | tf_op jit(solution)/shard_map/ppermute | solution.py:19
  49.3 14.2 %copy-start.23 = (bf16[2,48,16,1,1,16]{1,5,2,0,4,3:T(8,128)(2,1)S(1)}, bf16[2,48,16,1,1,16]{1,5,2,0,4,3:T(8,128)(2,1)}, u32[]{:S(2)}) copy-start(bf16[2,48,16,1,1,16]{1,5,2,0,4,3:T(8,128)(2,1)} %copy-done.22) | copy-start | bytes 147460
  49.3 14.2 %copy-start.25 = (bf16[2,48,16,1,1,16]{1,5,2,0,4,3:T(8,128)(2,1)S(1)}, bf16[2,48,16,1,1,16]{1,5,2,0,4,3:T(8,128)(2,1)}, u32[]{:S(2)}) copy-start(bf16[2,48,16,1,1,16]{1,5,2,0,4,3:T(8,128)(2,1)} %copy-done.24) | copy-start | bytes 147460
  49.3 14.2 %copy-start.27 = (bf16[2,48,16,1,1,16]{1,5,2,0,4,3:T(8,128)(2,1)S(1)}, bf16[2,48,16,1,1,16]{1,5,2,0,4,3:T(8,128)(2,1)}, u32[]{:S(2)}) copy-start(bf16[2,48,16,1,1,16]{1,5,2,0,4,3:T(8,128)(2,1)} %copy-done.26) | copy-start | bytes 147460
  61.7 5.2 copy-start.4
  61.7 6.7 copy-start
  74.2 3.0 copy-start.30
  74.2 3.0 copy-start.32
  77.2 3.8 copy-start.13
  153.9 24.7 %copy-start.1 = (f32[2,48,16,1,1,16]{1,5,2,0,4,3:T(8,128)}, f32[2,48,16,1,1,16]{1,5,2,0,4,3:T(8,128)S(1)}, u32[]{:S(2)}) copy-start(f32[2,48,16,1,1,16]{1,5,2,0,4,3:T(8,128)S(1)} %get-tuple-element.41) | copy-start | bytes 294916
  154.0 6.9 collective-permute-start.5
  155.9 8.1 %collective-permute-start.4 = (bf16[2,48,16,1,1,16]{1,5,2,0,4,3:T(8,128)(2,1)S(1)}, bf16[2,48,16,1,1,16]{1,5,2,0,4,3:T(8,128)(2,1)S(1)}, u32[]{:S(2)}, u32[]{:S(2)}) collective-permute-start(bf16[2,48,16,1,1,16]{1,5,2,0,4,3:T(8,128)(2,1)S(1)} %get-tuple-element.40), channel_id=1, source_target_pairs={{0,4},{4,8},{8,12},{12,16},{16,20},{20,24},{24,28},{28,0},{1,5},{5... | collective-permute-start | bytes 147464 | tf_op jit(solution)/shard_map/ppermute | solution.py:19
  164.1 9.8 %collective-permute-start.7 = (bf16[2,48,16,3,1,16]{1,5,2,0,4,3:T(8,128)(2,1)S(1)}, bf16[2,48,16,3,1,16]{1,5,2,0,4,3:T(8,128)(2,1)S(1)}, u32[]{:S(2)}, u32[]{:S(2)}) collective-permute-start(bf16[2,48,16,3,1,16]{1,5,2,0,4,3:T(8,128)(2,1)S(1)} %pad_maximum_fusion.1), channel_id=1, source_target_pairs={{1,0},{2,1},{3,2},{0,3},{5,4},{6,5},{7,6},{4,7},{9,8},{10,9},{11,1... | collective-permute-start | bytes 442376 | tf_op jit(solution)/shard_map/ppermute | solution.py:21
  167.5 11.0 %collective-permute-start.6 = (bf16[2,48,16,3,1,16]{1,5,2,0,4,3:T(8,128)(2,1)S(1)}, bf16[2,48,16,3,1,16]{1,5,2,0,4,3:T(8,128)(2,1)S(1)}, u32[]{:S(2)}, u32[]{:S(2)}) collective-permute-start(bf16[2,48,16,3,1,16]{1,5,2,0,4,3:T(8,128)(2,1)S(1)} %pad_maximum_fusion.1), channel_id=1, source_target_pairs={{0,1},{1,2},{2,3},{3,0},{4,5},{5,6},{6,7},{7,4},{8,9},{9,10},{10,1... | collective-permute-start | bytes 442376 | tf_op jit(solution)/shard_map/ppermute | solution.py:19
  333.7 23.6 %copy-start.5 = (f32[2,48,16,1,1,16]{1,5,2,0,4,3:T(8,128)}, f32[2,48,16,1,1,16]{1,5,2,0,4,3:T(8,128)S(1)}, u32[]{:S(2)}) copy-start(f32[2,48,16,1,1,16]{1,5,2,0,4,3:T(8,128)S(1)} %get-tuple-element.39) | copy-start | bytes 294916
  333.7 6.9 collective-permute-start.9
  335.7 8.1 %collective-permute-start.8 = (bf16[2,48,16,1,1,16]{1,5,2,0,4,3:T(8,128)(2,1)S(1)}, bf16[2,48,16,1,1,16]{1,5,2,0,4,3:T(8,128)(2,1)S(1)}, u32[]{:S(2)}, u32[]{:S(2)}) collective-permute-start(bf16[2,48,16,1,1,16]{1,5,2,0,4,3:T(8,128)(2,1)S(1)} %get-tuple-element.38), channel_id=1, source_target_pairs={{0,4},{4,8},{8,12},{12,16},{16,20},{20,24},{24,28},{28,0},{1,5},{5... | collective-permute-start | bytes 147464 | tf_op jit(solution)/shard_map/ppermute | solution.py:19
  343.9 9.7 %collective-permute-start.11 = (bf16[2,48,16,3,1,16]{1,5,2,0,4,3:T(8,128)(2,1)S(1)}, bf16[2,48,16,3,1,16]{1,5,2,0,4,3:T(8,128)(2,1)S(1)}, u32[]{:S(2)}, u32[]{:S(2)}) collective-permute-start(bf16[2,48,16,3,1,16]{1,5,2,0,4,3:T(8,128)(2,1)S(1)} %pad_maximum_fusion.2), channel_id=1, source_target_pairs={{1,0},{2,1},{3,2},{0,3},{5,4},{6,5},{7,6},{4,7},{9,8},{10,9},{11,1... | collective-permute-start | bytes 442376 | tf_op jit(solution)/shard_map/ppermute | solution.py:21
  346.2 10.9 %collective-permute-start.10 = (bf16[2,48,16,3,1,16]{1,5,2,0,4,3:T(8,128)(2,1)S(1)}, bf16[2,48,16,3,1,16]{1,5,2,0,4,3:T(8,128)(2,1)S(1)}, u32[]{:S(2)}, u32[]{:S(2)}) collective-permute-start(bf16[2,48,16,3,1,16]{1,5,2,0,4,3:T(8,128)(2,1)S(1)} %pad_maximum_fusion.2), channel_id=1, source_target_pairs={{0,1},{1,2},{2,3},{3,0},{4,5},{5,6},{6,7},{7,4},{8,9},{9,10},{10,1... | collective-permute-start | bytes 442376 | tf_op jit(solution)/shard_map/ppermute | solution.py:19
  362.3 2.5 copy-start.35
  435.4 5.1 copy-start.6
  436.2 3.2 copy-start.50
  436.2 3.2 copy-start.52
  516.6 24.6 %copy-start.8 = (f32[2,48,16,1,1,16]{1,5,2,0,4,3:T(8,128)}, f32[2,48,16,1,1,16]{1,5,2,0,4,3:T(8,128)S(1)}, u32[]{:S(2)}) copy-start(f32[2,48,16,1,1,16]{1,5,2,0,4,3:T(8,128)S(1)} %get-tuple-element.37) | copy-start | bytes 294916
  516.6 6.9 collective-permute-start.13
  518.6 8.1 %collective-permute-start.12 = (bf16[2,48,16,1,1,16]{1,5,2,0,4,3:T(8,128)(2,1)S(1)}, bf16[2,48,16,1,1,16]{1,5,2,0,4,3:T(8,128)(2,1)S(1)}, u32[]{:S(2)}, u32[]{:S(2)}) collective-permute-start(bf16[2,48,16,1,1,16]{1,5,2,0,4,3:T(8,128)(2,1)S(1)} %get-tuple-element.36), channel_id=1, source_target_pairs={{0,4},{4,8},{8,12},{12,16},{16,20},{20,24},{24,28},{28,0},{1,5},{5... | collective-permute-start | bytes 147464 | tf_op jit(solution)/shard_map/ppermute | solution.py:19
  526.7 9.7 %collective-permute-start.15 = (bf16[2,48,16,3,1,16]{1,5,2,0,4,3:T(8,128)(2,1)S(1)}, bf16[2,48,16,3,1,16]{1,5,2,0,4,3:T(8,128)(2,1)S(1)}, u32[]{:S(2)}, u32[]{:S(2)}) collective-permute-start(bf16[2,48,16,3,1,16]{1,5,2,0,4,3:T(8,128)(2,1)S(1)} %pad_maximum_fusion.3), channel_id=1, source_target_pairs={{1,0},{2,1},{3,2},{0,3},{5,4},{6,5},{7,6},{4,7},{9,8},{10,9},{11,1... | collective-permute-start | bytes 442376 | tf_op jit(solution)/shard_map/ppermute | solution.py:21
  529.8 11.1 %collective-permute-start.14 = (bf16[2,48,16,3,1,16]{1,5,2,0,4,3:T(8,128)(2,1)S(1)}, bf16[2,48,16,3,1,16]{1,5,2,0,4,3:T(8,128)(2,1)S(1)}, u32[]{:S(2)}, u32[]{:S(2)}) collective-permute-start(bf16[2,48,16,3,1,16]{1,5,2,0,4,3:T(8,128)(2,1)S(1)} %pad_maximum_fusion.3), channel_id=1, source_target_pairs={{0,1},{1,2},{2,3},{3,0},{4,5},{5,6},{6,7},{7,4},{8,9},{9,10},{10,1... | collective-permute-start | bytes 442376 | tf_op jit(solution)/shard_map/ppermute | solution.py:19
  546.2 73.1 %copy-start.31 = (f32[1,48,256]{1,2,0:T(8,128)S(1)}, f32[1,48,256]{1,2,0:T(8,128)}, u32[]{:S(2)}) copy-start(f32[1,48,256]{1,2,0:T(8,128)} %get-tuple-element.108) | copy-start | bytes 147460
  546.2 73.1 %copy-start.33 = (f32[1,48,256]{1,2,0:T(8,128)S(1)}, f32[1,48,256]{1,2,0:T(8,128)}, u32[]{:S(2)}) copy-start(f32[1,48,256]{1,2,0:T(8,128)} %get-tuple-element.109) | copy-start | bytes 147460
  546.2 73.1 %copy-start.43 = (f32[16]{0:T(128)S(1)}, f32[16]{0:T(128)}, u32[]{:S(2)}) copy-start(f32[16]{0:T(128)} %copy-done.42) | copy-start | bytes 196
  546.2 73.1 %copy-start.45 = (f32[16]{0:T(128)S(1)}, f32[16]{0:T(128)}, u32[]{:S(2)}) copy-start(f32[16]{0:T(128)} %copy-done.44) | copy-start | bytes 196
  546.2 73.1 %copy-start.47 = (f32[16]{0:T(128)S(1)}, f32[16]{0:T(128)}, u32[]{:S(2)}) copy-start(f32[16]{0:T(128)} %copy-done.46) | copy-start | bytes 196
  546.2 73.1 %copy-start.49 = (f32[16]{0:T(128)S(1)}, f32[16]{0:T(128)}, u32[]{:S(2)}) copy-start(f32[16]{0:T(128)} %copy-done.48) | copy-start | bytes 196
  546.2 73.1 %copy-start.51 = (f32[16]{0:T(128)S(1)}, f32[16]{0:T(128)}, u32[]{:S(2)}) copy-start(f32[16]{0:T(128)} %copy-done.50) | copy-start | bytes 196
  546.2 73.1 %copy-start.53 = (f32[16]{0:T(128)S(1)}, f32[16]{0:T(128)}, u32[]{:S(2)}) copy-start(f32[16]{0:T(128)} %copy-done.52) | copy-start | bytes 196
  546.2 73.3 %copy-start.2 = (f32[2,48,16,1,1,16]{1,5,2,0,4,3:T(8,128)S(1)}, f32[2,48,16,1,1,16]{1,5,2,0,4,3:T(8,128)}, u32[]{:S(2)}) copy-start(f32[2,48,16,1,1,16]{1,5,2,0,4,3:T(8,128)} %copy-done.1) | copy-start | bytes 294916
  548.7 71.0 %copy-start.55 = (f32[16]{0:T(128)S(1)}, f32[16]{0:T(128)}, u32[]{:S(2)}) copy-start(f32[16]{0:T(128)} %copy-done.54) | copy-start | bytes 196
  548.8 71.0 %copy-start.57 = (f32[16]{0:T(128)S(1)}, f32[16]{0:T(128)}, u32[]{:S(2)}) copy-start(f32[16]{0:T(128)} %copy-done.56) | copy-start | bytes 196
  620.9 73.8 %copy-start.29 = (bf16[2,24,2,2,3,512]{5,3,2,4,1,0:T(2,128)(2,1)S(1)}, bf16[2,24,2,2,3,512]{5,3,2,4,1,0:T(2,128)(2,1)}, u32[]{:S(2)}) copy-start(bf16[2,24,2,2,3,512]{5,3,2,4,1,0:T(2,128)(2,1)} %copy-done.28) | copy-start | bytes 1769476
  (26 other events, 37.5 us)
where the time goes:
time: 698 us; the launch traced here: 697 us
  blocking collectives  517 us (74%)
  starting transfers between devices  51.1 us (7%)
  waiting for transfers between devices  46.8 us (7%)
  matrix products  37.1 us (5%)
  other arithmetic  32.9 us (5%)
  local copies, waits for them, and re-layouts  10.3 us (1%)
    psum x4, blocking collectives, lengths(): return lax.psum(values, ('gz', 'gy'))  286 us
    psum x3, blocking collectives, projections(): return lax.psum(values, ('gz', 'gy'))  210 us
    dot_general x16, matrix products, contract(): return jnp.einsum('tzymij,mjtzyr->itzyr', left, right, precision=HIGH)  34.8 us
    ppermute x8, waiting for transfers between devices, extended(): lax.ppermute(tail, axis, [(i, (i + 1) % count) for i in range(count)])  29.1 us
    ppermute x8, starting transfers between devices, extended(): lax.ppermute(head, axis, [((i + 1) % count, i) for i in range(count)])  26.4 us
    ppermute x8, starting transfers between devices, extended(): lax.ppermute(tail, axis, [(i, (i + 1) % count) for i in range(count)])  24.7 us
    all_gather x1, blocking collectives, body(): right = lax.all_gather(right, 'ta', axis=2, tiled=True)  20.6 us
    ppermute x8, waiting for transfers between devices, extended(): lax.ppermute(head, axis, [((i + 1) % count, i) for i in range(count)])  17.6 us
  transfers between devices with their start and end apart: 16, of which 15 were waited for; matrix products, arithmetic and copies ran while one was open for 1% of the time, Pallas kernels for 0%

commit v1 on v0

v1 whole, which is shorter than its diff:
```python
import functools

import jax
import jax.numpy as jnp
from jax import lax
from jax.experimental import pallas as pl
from jax.experimental.pallas import tpu as pltpu
from jax.sharding import PartitionSpec as P

MESH = pl.DeviceIdType.MESH
F32 = jnp.float32
BF16 = jnp.bfloat16
CDOF = 48
NVEC = 24
NRHS = 16
LINKS = 9
LANES = 128


def lane_iota(shape):
    return lax.broadcasted_iota(jnp.int32, shape, len(shape) - 1)


def group_of(shape):
    return lax.rem(lax.div(lane_iota(shape), NRHS), 4)


def sign_of(shape):
    return jnp.where(lane_iota(shape) < 64, -1.0, 1.0).astype(F32)


def times_i(field):
    return sign_of(field.shape) * pltpu.roll(field, 64, 1)


def restrict(nv_ref, res_ref, rows_ref):
    total = None
    for colour in range(3):
        basis = nv_ref[:, :, colour].reshape(2 * NVEC * 4, 512)
        source = res_ref[:, :, colour].reshape(2 * 4 * NRHS, 512)
        part = lax.dot_general(basis, source, (((1,), (1,)), ((), ())), preferred_element_type=F32)
        total = part if total is None else total + part
    rows_ref[...] = total
    by_spin = [rows_ref[pl.ds(s, 2 * NVEC, stride=4), :] for s in range(4)]
    group = group_of((2 * NVEC, LANES))
    halves = []
    for chirality in range(2):
        a, b = 2 * chirality, 2 * chirality + 1
        picked = jnp.where(group == a, by_spin[a], jnp.where(group == b, by_spin[b], 0.0))
        picked = picked + pltpu.roll(picked, LANES - NRHS, 1)
        if chirality == 1:
            picked = pltpu.roll(picked, LANES - 2 * NRHS, 1)
        halves.append(picked[:NVEC] - times_i(picked[NVEC:]))
    field = jnp.concatenate(halves, axis=0)
    return jnp.where(group == 0, field, 0.0)


def packed(field):
    high = field.astype(BF16).astype(F32)
    return (high + pltpu.roll(field - high, 2 * NRHS, 1)).astype(BF16)


def apply_links(links, cells):
    product = jnp.dot(links, cells, preferred_element_type=F32)
    value = product[:CDOF] + times_i(product[CDOF:])
    value = value + pltpu.roll(value, LANES - 2 * NRHS, 1)
    return jnp.where(group_of(value.shape) == 0, value, 0.0)


def row_sum(product):
    return jnp.sum(product, axis=0, keepdims=True)


def cmul(a, b):
    return a[0] * b[0] - a[1] * b[1], a[0] * b[1] + a[1] * b[0]


def cmul_conj(a, b):
    return a[0] * b[0] + a[1] * b[1], a[0] * b[1] - a[1] * b[0]


def csub(a, b):
    return a[0] - b[0], a[1] - b[1]


def solve(diag, upper, right):
    n = len(diag)
    d, inv, low = [], [], {}
    for j in range(n):
        value = diag[j]
        for k in range(j):
            value = value - d[k] * (low[j, k][0] ** 2 + low[j, k][1] ** 2)
        d.append(value)
        inv.append(1.0 / value)
        for i in range(j + 1, n):
            entry = (upper[j, i][0], -upper[j, i][1])
            for k in range(j):
                term = cmul_conj(low[j, k], low[i, k])
                entry = csub(entry, (d[k] * term[0], d[k] * term[1]))
            low[i, j] = (entry[0] * inv[j], entry[1] * inv[j])
    y = []
    for i in range(n):
        value = right[i]
        for k in range(i):
            value = csub(value, cmul(low[i, k], y[k]))
        y.append(value)
    c = [None] * n
    for i in reversed(range(n)):
        value = (y[i][0] * inv[i], y[i][1] * inv[i])
        for k in range(i + 1, n):
            value = csub(value, cmul_conj(low[k, i], c[k]))
        c[i] = value
    return c


def both_halves(row):
    row = jnp.where(lane_iota(row.shape) < NRHS, row, 0.0)
    return row + pltpu.roll(row, 64, 1)


def all_to_all(shape, me, peers, value, buf, send_sem, recv_sem):
    buf[me] = value
    for peer in peers:
        pltpu.make_async_remote_copy(
            src_ref=buf.at[me],
            dst_ref=buf.at[me],
            send_sem=send_sem,
            recv_sem=recv_sem,
            device_id=peer,
            device_id_type=MESH,
        ).start()


def all_wait(count, peer, buf, send_sem, recv_sem):
    block = buf.at[pl.ds(0, count)]
    arrived = pltpu.make_async_remote_copy(
        src_ref=block, dst_ref=block, send_sem=send_sem, recv_sem=recv_sem, device_id=peer, device_id_type=MESH
    )
    arrived.wait_recv()
    arrived.wait_send()


def coarse_kernel(
    sizes,
    res_hbm,
    nv_hbm,
    op_hbm,
    x_ref,
    r_ref,
    res_v,
    nv_v,
    op_v,
    col_v,
    rows_v,
    cells,
    theta_buf,
    t_buf,
    zx_buf,
    local_sem,
    halo_send,
    halo_recv,
    sum_send,
    sum_recv,
):
    nt, nz, nx = sizes
    t, z, x = lax.axis_index("ta"), lax.axis_index("gz"), lax.axis_index("gy")
    loads = [
        pltpu.make_async_copy(op_hbm.at[t, 0, 0], op_v, local_sem.at[0]),
        pltpu.make_async_copy(op_hbm.at[:, 0, 0, 0], col_v, local_sem.at[1]),
        pltpu.make_async_copy(res_hbm, res_v, local_sem.at[2]),
        pltpu.make_async_copy(nv_hbm, nv_v, local_sem.at[3]),
    ]
    for load in loads:
        load.start()
    t_peers = [(lax.rem(t + d, nt), z, x) for d in range(1, nt)]
    zx_peers = [
        (t, lax.rem(z + a, nz), lax.rem(x + b, nx)) for a in range(nz) for b in range(nx) if (a, b) != (0, 0)
    ]
    barrier = pltpu.get_barrier_semaphore()
    for peer in t_peers + zx_peers:
        pl.semaphore_signal(barrier, inc=1, device_id=peer, device_id_type=MESH)

    loads[1].wait()
    eye = lax.broadcasted_iota(jnp.int32, (CDOF, CDOF), 0) == lax.broadcasted_iota(jnp.int32, (CDOF, CDOF), 1)
    trace = [jnp.zeros((CDOF, CDOF), F32), jnp.zeros((CDOF, CDOF), F32)]
    square = jnp.zeros((CDOF, CDOF), F32)
    for slab in range(nt):
        for part in range(2):
            block = col_v[slab, part].astype(F32)
            trace[part] = trace[part] + block
            square = square + block * block
    scale = 1.0 / (nt * nz * nx * CDOF)
    stats = [jnp.where(eye, trace[0], 0.0), jnp.where(eye, trace[1], 0.0), square]
    stats = [jnp.sum(row_sum(value), axis=1, keepdims=True) * scale for value in stats]
    stats = jnp.concatenate([jnp.broadcast_to(value, (1, LANES)) for value in stats], axis=0)

    loads[0].wait()
    links = jnp.concatenate(
        [
            jnp.concatenate([op_v[m, part].astype(F32) for m in range(LINKS)], axis=1)
            for part in range(2)
        ],
        axis=0,
    ).astype(BF16)

    loads[2].wait()
    loads[3].wait()
    start = restrict(nv_v, res_v, rows_v)
    pl.semaphore_wait(barrier, len(t_peers) + len(zx_peers))

    slots = [
        (1, (lax.rem(t + nt - 1, nt), z, x)),
        (2, (lax.rem(t + 1, nt), z, x)),
        (3, (t, lax.rem(z + nz - 1, nz), x)),
        (4, (t, lax.rem(z + 1, nz), x)),
        (5, (t, z, lax.rem(x + nx - 1, nx))),
        (6, (t, z, lax.rem(x + 1, nx))),
    ]
    me_zx = z * nx + x
    powers = [start]
    for k in range(4):
        own = packed(powers[k])
        cells[k, 0] = own
        for m, peer in slots:
            pltpu.make_async_remote_copy(
                src_ref=cells.at[k, 0],
                dst_ref=cells.at[k, m],
                send_sem=halo_send.at[k],
                recv_sem=halo_recv.at[k],
                device_id=peer,
                device_id_type=MESH,
            ).start()
        cells[k, 7] = own
        cells[k, 8] = own
        if k == 0:
            all_to_all(None, me_zx, zx_peers, stats, theta_buf, sum_send.at[0], sum_recv.at[0])
        six = cells.at[k, pl.ds(1, 6)]
        arrived = pltpu.make_async_remote_copy(
            src_ref=six,
            dst_ref=six,
            send_sem=halo_send.at[k],
            recv_sem=halo_recv.at[k],
            device_id=slots[0][1],
            device_id_type=MESH,
        )
        arrived.wait_recv()
        arrived.wait_send()
        powers.append(apply_links(links, cells[k].reshape(LINKS * CDOF, LANES)))

    all_wait(nz * nx - 1, zx_peers[0], theta_buf, sum_send.at[0], sum_recv.at[0])
    stats = jnp.sum(theta_buf[...], axis=0)
    square = stats[2:3]
    inverse = jnp.where(square > 0.0, lax.rsqrt(jnp.where(square > 0.0, square, 1.0)), 1.0)
    theta = (stats[0:1] * inverse, stats[1:2] * inverse)

    level = []
    weight = None
    for k in range(5):
        level.append(powers[k] if k == 0 else powers[k] * weight)
        weight = inverse if weight is None else weight * inverse
    basis = [level[0]]
    for _ in range(4):
        level = [
            level[i + 1] - theta[0] * level[i] - theta[1] * times_i(level[i]) for i in range(len(level) - 1)
        ]
        basis.append(level[0])
    images = [
        basis[k + 1] + theta[0] * basis[k] + theta[1] * times_i(basis[k]) for k in range(4)
    ]
    turned = [times_i(image) for image in images]
    start_turned = times_i(start)

    pairs = [(i, j) for i in range(4) for j in range(i + 1, 4)]
    rows = [row_sum(images[k] * images[k]) for k in range(4)]
    rows += [row_sum(images[k] * start) for k in range(4)]
    rows += [row_sum(turned[k] * start) for k in range(4)]
    rows += [row_sum(images[i] * images[j]) for i, j in pairs]
    rows += [row_sum(turned[i] * images[j]) for i, j in pairs]
    table = jnp.concatenate(rows, axis=0)
    table = table + pltpu.roll(table, 64, 1)
    table = jnp.where(lane_iota(table.shape) < NRHS, table, 0.0)
    dense = jnp.concatenate(
        [
            row_sum(pltpu.roll(table[8 * g : 8 * g + 8], 0, 1, stride=NRHS, stride_axis=0))
            for g in range(3)
        ],
        axis=0,
    )

    all_to_all(None, t, t_peers, dense, t_buf, sum_send.at[1], sum_recv.at[1])
    all_wait(nt - 1, t_peers[0], t_buf, sum_send.at[1], sum_recv.at[1])
    dense = jnp.sum(t_buf[...], axis=0)
    all_to_all(None, me_zx, zx_peers, dense, zx_buf, sum_send.at[2], sum_recv.at[2])
    all_wait(nz * nx - 1, zx_peers[0], zx_buf, sum_send.at[2], sum_recv.at[2])
    dense = jnp.sum(zx_buf[...], axis=0)

    sums = []
    for g in range(3):
        spread = pltpu.roll(
            jnp.broadcast_to(dense[g : g + 1], (8, LANES)), 0, 1, stride=NRHS, stride_axis=0
        )
        sums += [spread[(8 - i) % 8 : (8 - i) % 8 + 1] for i in range(8)]
    diag = sums[0:4]
    right = [(sums[4 + k], sums[8 + k]) for k in range(4)]
    upper = {pair: (sums[12 + n], sums[18 + n]) for n, pair in enumerate(pairs)}
    coef = [(both_halves(c[0]), both_halves(c[1])) for c in solve(diag, upper, right)]

    field = None
    remain = start
    for k in range(4):
        cr, ci = coef[k]
        term = (cr * basis[k] + ci * times_i(basis[k])) * inverse
        field = term if field is None else field + term
        remain = remain - cr * images[k] - ci * turned[k]
    x_ref[...] = field
    r_ref[...] = remain


def prolong_kernel(x_ref, r_ref, nv_ref, out_ref, remain_ref, rows_v):
    x = x_ref[...].astype(BF16).astype(F32)
    upper, lower = x[:NVEC], x[NVEC:]
    every = upper + pltpu.roll(upper, NRHS, 1) + pltpu.roll(lower, 2 * NRHS, 1) + pltpu.roll(lower, 3 * NRHS, 1)
    every = jnp.concatenate([every, times_i(every)], axis=0)
    group = group_of(every.shape)
    for s in range(4):
        rows_v[pl.ds(s, 2 * NVEC, stride=4), :] = jnp.where(group == s, every, 0.0)
    weights = rows_v[...].T.astype(BF16)
    for colour in range(3):
        basis = nv_ref[:, :, colour].reshape(2 * NVEC * 4, 512)
        value = jnp.dot(weights, basis, preferred_element_type=F32)
        out_ref[:, :, colour] = value.astype(BF16).reshape(2, 4, NRHS, 512)
    turned = r_ref[...].T
    remain_ref[0] = turned[0:NRHS]
    remain_ref[1] = turned[64 : 64 + NRHS]


def body(sizes, residual, null_vectors, coarse_op):
    sites = residual.shape[-1]
    res = residual.reshape(2, 4, 3, NRHS, sites)
    nv = null_vectors.transpose(0, 1, 3, 4, 5, 6, 2, 7).reshape(2, NVEC, 3, 4, sites)
    nt, nz, nx = sizes
    any_spec = pl.BlockSpec(memory_space=pltpu.HBM)
    vmem_spec = pl.BlockSpec(memory_space=pltpu.VMEM)
    field = jax.ShapeDtypeStruct((CDOF, LANES), F32)
    x, r = pl.pallas_call(
        functools.partial(coarse_kernel, sizes),
        out_shape=(field, field),
        in_specs=[any_spec] * 3,
        out_specs=(vmem_spec, vmem_spec),
        scratch_shapes=[
            pltpu.VMEM(res.shape, BF16),
            pltpu.VMEM(nv.shape, BF16),
            pltpu.VMEM((LINKS, 2, CDOF, CDOF), BF16),
            pltpu.VMEM((nt, 2, CDOF, CDOF), BF16),
            pltpu.VMEM((2 * NVEC * 4, LANES), F32),
            pltpu.VMEM((4, LINKS, CDOF, LANES), BF16),
            pltpu.VMEM((nz * nx, 3, LANES), F32),
            pltpu.VMEM((nt, 3, LANES), F32),
            pltpu.VMEM((nz * nx, 3, LANES), F32),
            pltpu.SemaphoreType.DMA((4,)),
            pltpu.SemaphoreType.DMA((4,)),
            pltpu.SemaphoreType.DMA((4,)),
            pltpu.SemaphoreType.DMA((3,)),
            pltpu.SemaphoreType.DMA((3,)),
        ],
        compiler_params=pltpu.CompilerParams(
            collective_id=0, has_side_effects=True, vmem_limit_bytes=16 * 1024 * 1024
        ),
    )(res, nv, coarse_op)
    correction, remain = pl.pallas_call(
        prolong_kernel,
        out_shape=(
            jax.ShapeDtypeStruct((2, 4, 3, NRHS, sites), BF16),
            jax.ShapeDtypeStruct((2, NRHS, CDOF), F32),
        ),
        in_specs=[vmem_spec] * 3,
        out_specs=(vmem_spec, vmem_spec),
        scratch_shapes=[pltpu.VMEM((2 * NVEC * 4, LANES), F32)],
        compiler_params=pltpu.CompilerParams(vmem_limit_bytes=16 * 1024 * 1024),
    )(x, r, nv)
    correction = correction.reshape(2, 4, 3, NRHS, 1, 1, 1, sites)
    remain = remain.transpose(0, 2, 1).reshape(2, CDOF, 1, 1, 1, NRHS)
    return correction, remain


def solution(mesh):
    sizes = (mesh.shape["ta"], mesh.shape["gz"], mesh.shape["gy"])
    return jax.shard_map(
        functools.partial(body, sizes),
        mesh=mesh,
        in_specs=(
            P(None, None, None, None, "ta", "gz", "gy", None),
            P(None, None, None, None, "ta", "gz", "gy", None),
            P(None, "gz", "gy", None, None, None, None),
        ),
        out_specs=(
            P(None, None, None, None, "ta", "gz", "gy", None),
            P(None, None, "ta", "gz", "gy", None),
        ),
        check_vma=False,
    )
```

time: 698 us -> 50.4 us (0.07)
  the two profiles are of different devices: /device:TPU:8 before, /device:TPU:1 now
where the time goes in v1:
time: 50.4 us; the launch traced here: 50.2 us
  Pallas kernels  45.4 us (90%)
  local copies, waits for them, and re-layouts  4.06 us (8%)
  between operations  0.66 us (1%)
    pallas_call x1, Pallas kernels, body(): pl.pallas_call(functools.partial(coarse_kernel, sizes), out_shape=(field,...  44.2 us
    unnamed x8, local copies, waits for them, and re-layouts  4.06 us
    pallas_call x1, Pallas kernels, body(): pl.pallas_call(prolong_kernel, out_shape=(jax.ShapeDtypeStruct((2, 4, 3,...  1.21 us

profile of v1, /device:TPU:1, one launch (start us, length us, event | category | flops | bytes accessed | tf_op | source)
XLA Modules:
  0.0 50.2 jit_solution(10199704002674871016)
XLA Ops:
  0.6 0.0 copy-start
  0.6 2.0 %copy-done = bf16[16,1,1,9,2,48,48]{6,5,4,3,2,1,0:T(8,128)(2,1)S(1)} copy-done((bf16[16,1,1,9,2,48,48]{6,5,4,3,2,1,0:T(8,128)(2,1)S(1)}, bf16[16,1,1,9,2,48,48]{6,5,4,3,2,1,0:T(8,128)(2,1)}, u32[]{:S(2)}) %copy-start) | copy-done | bytes 1327128
  2.6 0.0 copy-start.1
  2.6 1.1 %copy-done.1 = bf16[2,24,4,3,1,1,1,512]{7,2,6,5,4,3,1,0:T(4,128)(2,1)S(1)} copy-done((bf16[2,24,4,3,1,1,1,512]{7,2,6,5,4,3,1,0:T(4,128)(2,1)S(1)}, bf16[2,24,4,3,1,1,1,512]{7,2,6,5,4,3,1,0:T(4,128)(2,1)}, u32[]{:S(2)}) %copy-start.1) | copy-done | bytes 589848
  3.7 0.0 copy-start.3
  3.7 1.0 %copy-done.3 = bf16[2,4,3,16,1,1,1,512]{7,3,6,5,4,2,1,0:T(8,128)(2,1)S(1)} copy-done((bf16[2,4,3,16,1,1,1,512]{7,3,6,5,4,2,1,0:T(8,128)(2,1)S(1)}, bf16[2,4,3,16,1,1,1,512]{7,3,6,5,4,2,1,0:T(8,128)(2,1)}, u32[]{:S(2)}) %copy-start.3) | copy-done | bytes 393240
  4.7 0.0 copy-start.2
  4.7 44.2 %shard_map.50 = (f32[48,128]{1,0:T(8,128)S(1)}, f32[48,128]{1,0:T(8,128)S(1)}) custom-call(bf16[2,4,3,16,512]{4,3,2,1,0:T(8,128)(2,1)S(1)} %bitcast.16, bf16[2,24,3,4,512]{4,3,2,1,0:T(4,128)(2,1)S(1)} %bitcast.14, bf16[16,1,1,9,2,48,48]{6,5,4,3,2,1,0:T(8,128)(2,1)S(1)} %copy-done), custom_call_target="tpu_custom_call" | custom-call | tf_op jit(solution)/shard_map/pallas_call | solution.py:345
  48.9 0.0 copy-done.2
  49.0 1.2 %shard_map.51 = (bf16[2,4,3,16,512]{4,3,2,1,0:T(8,128)(2,1)}, f32[2,16,48]{2,1,0:T(8,128)}) custom-call(f32[48,128]{1,0:T(8,128)S(1)} %get-tuple-element.6.x_ref, f32[48,128]{1,0:T(8,128)S(1)} %get-tuple-element.7.r_ref, bf16[2,24,3,4,512]{4,3,2,1,0:T(4,128)(2,1)S(1)} %bitcast.15), custom_call_target="tpu_custom_call" | custom-call | tf_op jit(solution)/shard_map/pallas_call | solution.py:370
Async XLA Ops:
  0.6 2.0 %copy-start = (bf16[16,1,1,9,2,48,48]{6,5,4,3,2,1,0:T(8,128)(2,1)S(1)}, bf16[16,1,1,9,2,48,48]{6,5,4,3,2,1,0:T(8,128)(2,1)}, u32[]{:S(2)}) copy-start(bf16[16,1,1,9,2,48,48]{6,5,4,3,2,1,0:T(8,128)(2,1)} %op_hbm.1) | copy-start | bytes 3981316
  2.6 1.1 %copy-start.1 = (bf16[2,24,4,3,1,1,1,512]{7,2,6,5,4,3,1,0:T(4,128)(2,1)S(1)}, bf16[2,24,4,3,1,1,1,512]{7,2,6,5,4,3,1,0:T(4,128)(2,1)}, u32[]{:S(2)}) copy-start(bf16[2,24,4,3,1,1,1,512]{7,2,6,5,4,3,1,0:T(4,128)(2,1)} %param.4) | copy-start | bytes 1769476
  3.7 1.0 %copy-start.3 = (bf16[2,4,3,16,1,1,1,512]{7,3,6,5,4,2,1,0:T(8,128)(2,1)S(1)}, bf16[2,4,3,16,1,1,1,512]{7,3,6,5,4,2,1,0:T(8,128)(2,1)}, u32[]{:S(2)}) copy-start(bf16[2,4,3,16,1,1,1,512]{7,3,6,5,4,2,1,0:T(8,128)(2,1)} %param.3) | copy-start | bytes 1179652
  4.7 44.3 %copy-start.2 = (bf16[2,24,4,3,1,1,1,512]{7,2,6,5,4,3,1,0:T(4,128)(2,1)S(1)}, bf16[2,24,4,3,1,1,1,512]{7,2,6,5,4,3,1,0:T(4,128)(2,1)}, u32[]{:S(2)}) copy-start(bf16[2,24,4,3,1,1,1,512]{7,2,6,5,4,3,1,0:T(4,128)(2,1)} %param.4) | copy-start | bytes 1769476

commit v2 on v1

--- a/solution.py
+++ b/solution.py
@@ -118,7 +118,11 @@
     return row + pltpu.roll(row, 64, 1)
 
 
-def all_to_all(shape, me, peers, value, buf, send_sem, recv_sem):
+def others(count, me):
+    return [k + jnp.where(k >= me, 1, 0) for k in range(count - 1)]
+
+
+def send_to_all(me, peers, value, buf, send_sem, recv_sem):
     buf[me] = value
     for peer in peers:
         pltpu.make_async_remote_copy(
@@ -131,13 +135,10 @@
         ).start()
 
 
-def all_wait(count, peer, buf, send_sem, recv_sem):
-    block = buf.at[pl.ds(0, count)]
-    arrived = pltpu.make_async_remote_copy(
+def transfers(block, peer, send_sem, recv_sem):
+    return pltpu.make_async_remote_copy(
         src_ref=block, dst_ref=block, send_sem=send_sem, recv_sem=recv_sem, device_id=peer, device_id_type=MESH
     )
-    arrived.wait_recv()
-    arrived.wait_send()
 
 
 def coarse_kernel(
@@ -164,23 +165,69 @@
 ):
     nt, nz, nx = sizes
     t, z, x = lax.axis_index("ta"), lax.axis_index("gz"), lax.axis_index("gy")
+    me_zx = z * nx + x
     loads = [
-        pltpu.make_async_copy(op_hbm.at[t, 0, 0], op_v, local_sem.at[0]),
-        pltpu.make_async_copy(op_hbm.at[:, 0, 0, 0], col_v, local_sem.at[1]),
-        pltpu.make_async_copy(res_hbm, res_v, local_sem.at[2]),
-        pltpu.make_async_copy(nv_hbm, nv_v, local_sem.at[3]),
+        pltpu.make_async_copy(nv_hbm, nv_v, local_sem.at[0]),
+        pltpu.make_async_copy(res_hbm, res_v, local_sem.at[1]),
+        pltpu.make_async_copy(op_hbm.at[t, 0, 0], op_v, local_sem.at[2]),
+        pltpu.make_async_copy(op_hbm.at[:, 0, 0, 0], col_v, local_sem.at[3]),
     ]
-    for load in loads:
-        load.start()
-    t_peers = [(lax.rem(t + d, nt), z, x) for d in range(1, nt)]
-    zx_peers = [
-        (t, lax.rem(z + a, nz), lax.rem(x + b, nx)) for a in range(nz) for b in range(nx) if (a, b) != (0, 0)
+    slots = [
+        (3, (t, lax.rem(z + nz - 1, nz), x)),
+        (4, (t, lax.rem(z + 1, nz), x)),
+        (5, (t, z, lax.rem(x + nx - 1, nx))),
+        (6, (t, z, lax.rem(x + 1, nx))),
+        (1, (lax.rem(t + nt - 1, nt), z, x)),
+        (2, (lax.rem(t + 1, nt), z, x)),
+    ]
+    far = [(lax.rem(t + d, nt), z, x) for d in range(2, nt - 1)]
+    far += [
+        (t, lax.rem(z + a, nz), lax.rem(x + b, nx))
+        for a in range(nz)
+        for b in range(nx)
+        if (a, b) not in ((0, 0), (1, 0), (nz - 1, 0), (0, 1), (0, nx - 1))
     ]
     barrier = pltpu.get_barrier_semaphore()
-    for peer in t_peers + zx_peers:
+    for load in loads[:2]:
+        load.start()
+    for _, peer in slots:
         pl.semaphore_signal(barrier, inc=1, device_id=peer, device_id_type=MESH)
-
+    for load in loads[2:]:
+        load.start()
+    for peer in far:
+        pl.semaphore_signal(barrier, inc=1, device_id=peer, device_id_type=MESH)
+    t_peers = [(k, z, x) for k in others(nt, t)]
+    zx_peers = [(t, lax.div(k, nx), lax.rem(k, nx)) for k in others(nz * nx, me_zx)]
+
+    loads[0].wait()
     loads[1].wait()
+    start = restrict(nv_v, res_v, rows_v)
+    pl.semaphore_wait(barrier, len(slots) + len(far))
+
+    def send_halo(k, field):
+        own = packed(field)
+        cells[k, 0] = own
+        for m, peer in slots:
+            pltpu.make_async_remote_copy(
+                src_ref=cells.at[k, 0],
+                dst_ref=cells.at[k, m],
+                send_sem=halo_send.at[k],
+                recv_sem=halo_recv.at[k],
+                device_id=peer,
+                device_id_type=MESH,
+            ).start()
+        cells[k, 7] = own
+        cells[k, 8] = own
+
+    def halo(k):
+        return transfers(cells.at[k, pl.ds(1, 6)], slots[0][1], halo_send.at[k], halo_recv.at[k])
+
+    def sums_of(k, buf, count, peer):
+        return transfers(buf.at[pl.ds(0, count - 1)], peer, sum_send.at[k], sum_recv.at[k])
+
+    send_halo(0, start)
+
+    loads[3].wait()
     eye = lax.broadcasted_iota(jnp.int32, (CDOF, CDOF), 0) == lax.broadcasted_iota(jnp.int32, (CDOF, CDOF), 1)
     trace = [jnp.zeros((CDOF, CDOF), F32), jnp.zeros((CDOF, CDOF), F32)]
     square = jnp.zeros((CDOF, CDOF), F32)
@@ -193,8 +240,9 @@
     stats = [jnp.where(eye, trace[0], 0.0), jnp.where(eye, trace[1], 0.0), square]
     stats = [jnp.sum(row_sum(value), axis=1, keepdims=True) * scale for value in stats]
     stats = jnp.concatenate([jnp.broadcast_to(value, (1, LANES)) for value in stats], axis=0)
-
-    loads[0].wait()
+    send_to_all(me_zx, zx_peers, stats, theta_buf, sum_send.at[0], sum_recv.at[0])
+
+    loads[2].wait()
     links = jnp.concatenate(
         [
             jnp.concatenate([op_v[m, part].astype(F32) for m in range(LINKS)], axis=1)
@@ -203,80 +251,52 @@
         axis=0,
     ).astype(BF16)
 
-    loads[2].wait()
-    loads[3].wait()
-    start = restrict(nv_v, res_v, rows_v)
-    pl.semaphore_wait(barrier, len(t_peers) + len(zx_peers))
-
-    slots = [
-        (1, (lax.rem(t + nt - 1, nt), z, x)),
-        (2, (lax.rem(t + 1, nt), z, x)),
-        (3, (t, lax.rem(z + nz - 1, nz), x)),
-        (4, (t, lax.rem(z + 1, nz), x)),
-        (5, (t, z, lax.rem(x + nx - 1, nx))),
-        (6, (t, z, lax.rem(x + 1, nx))),
-    ]
-    me_zx = z * nx + x
     powers = [start]
-    for k in range(4):
-        own = packed(powers[k])
-        cells[k, 0] = own
-        for m, peer in slots:
-            pltpu.make_async_remote_copy(
-                src_ref=cells.at[k, 0],
-                dst_ref=cells.at[k, m],
-                send_sem=halo_send.at[k],
-                recv_sem=halo_recv.at[k],
-                device_id=peer,
-                device_id_type=MESH,
-            ).start()
-        cells[k, 7] = own
-        cells[k, 8] = own
-        if k == 0:
-            all_to_all(None, me_zx, zx_peers, stats, theta_buf, sum_send.at[0], sum_recv.at[0])
-        six = cells.at[k, pl.ds(1, 6)]
-        arrived = pltpu.make_async_remote_copy(
-            src_ref=six,
-            dst_ref=six,
-            send_sem=halo_send.at[k],
-            recv_sem=halo_recv.at[k],
-            device_id=slots[0][1],
-            device_id_type=MESH,
-        )
-        arrived.wait_recv()
-        arrived.wait_send()
+    for k in range(3):
+        halo(k).wait_recv()
         powers.append(apply_links(links, cells[k].reshape(LINKS * CDOF, LANES)))
-
-    all_wait(nz * nx - 1, zx_peers[0], theta_buf, sum_send.at[0], sum_recv.at[0])
+        send_halo(k + 1, powers[k + 1])
+
+    sums_of(0, theta_buf, nz * nx, zx_peers[0]).wait_recv()
     stats = jnp.sum(theta_buf[...], axis=0)
     square = stats[2:3]
     inverse = jnp.where(square > 0.0, lax.rsqrt(jnp.where(square > 0.0, square, 1.0)), 1.0)
     theta = (stats[0:1] * inverse, stats[1:2] * inverse)
-
-    level = []
-    weight = None
-    for k in range(5):
-        level.append(powers[k] if k == 0 else powers[k] * weight)
-        weight = inverse if weight is None else weight * inverse
-    basis = [level[0]]
-    for _ in range(4):
-        level = [
-            level[i + 1] - theta[0] * level[i] - theta[1] * times_i(level[i]) for i in range(len(level) - 1)
-        ]
+    weights = [inverse]
+    for _ in range(3):
+        weights.append(weights[-1] * inverse)
+
+    def times_theta(field):
+        return theta[0] * field + theta[1] * times_i(field)
+
+    level = [start] + [powers[k] * weights[k - 1] for k in range(1, 4)]
+    basis, last = [start], [times_theta(level[3])]
+    for _ in range(3):
+        level = [level[i + 1] - times_theta(level[i]) for i in range(len(level) - 1)]
         basis.append(level[0])
-    images = [
-        basis[k + 1] + theta[0] * basis[k] + theta[1] * times_i(basis[k]) for k in range(4)
-    ]
+        last.append(times_theta(level[-1]))
+    images = [basis[k + 1] + times_theta(basis[k]) for k in range(3)]
     turned = [times_i(image) for image in images]
     start_turned = times_i(start)
 
-    pairs = [(i, j) for i in range(4) for j in range(i + 1, 4)]
-    rows = [row_sum(images[k] * images[k]) for k in range(4)]
-    rows += [row_sum(images[k] * start) for k in range(4)]
-    rows += [row_sum(turned[k] * start) for k in range(4)]
-    rows += [row_sum(images[i] * images[j]) for i, j in pairs]
-    rows += [row_sum(turned[i] * images[j]) for i, j in pairs]
-    table = jnp.concatenate(rows, axis=0)
+    pairs = [(i, j) for j in range(4) for i in range(j)]
+    norms = [row_sum(images[k] * images[k]) for k in range(3)]
+    right = [row_sum(images[k] * start) for k in range(3)]
+    right_i = [row_sum(turned[k] * start) for k in range(3)]
+    cross = [row_sum(images[i] * images[j]) for i, j in pairs[:3]]
+    cross_i = [row_sum(turned[i] * images[j]) for i, j in pairs[:3]]
+
+    halo(3).wait_recv()
+    newest = apply_links(links, cells[3].reshape(LINKS * CDOF, LANES)) * weights[3]
+    for part in last:
+        newest = newest - part
+    images.append(newest + last[3])
+    norms.append(row_sum(images[3] * images[3]))
+    right.append(row_sum(images[3] * start))
+    right_i.append(-row_sum(images[3] * start_turned))
+    cross += [row_sum(images[i] * images[3]) for i in range(3)]
+    cross_i += [row_sum(turned[i] * images[3]) for i in range(3)]
+    table = jnp.concatenate(norms + right + right_i + cross + cross_i, axis=0)
     table = table + pltpu.roll(table, 64, 1)
     table = jnp.where(lane_iota(table.shape) < NRHS, table, 0.0)
     dense = jnp.concatenate(
@@ -287,18 +307,18 @@
         axis=0,
     )
 
-    all_to_all(None, t, t_peers, dense, t_buf, sum_send.at[1], sum_recv.at[1])
-    all_wait(nt - 1, t_peers[0], t_buf, sum_send.at[1], sum_recv.at[1])
+    send_to_all(t, t_peers, dense, t_buf, sum_send.at[1], sum_recv.at[1])
+    turned.append(times_i(images[3]))
+    basis_turned = [times_i(field) for field in basis]
+    sums_of(1, t_buf, nt, t_peers[0]).wait_recv()
     dense = jnp.sum(t_buf[...], axis=0)
-    all_to_all(None, me_zx, zx_peers, dense, zx_buf, sum_send.at[2], sum_recv.at[2])
-    all_wait(nz * nx - 1, zx_peers[0], zx_buf, sum_send.at[2], sum_recv.at[2])
+    send_to_all(me_zx, zx_peers, dense, zx_buf, sum_send.at[2], sum_recv.at[2])
+    sums_of(2, zx_buf, nz * nx, zx_peers[0]).wait_recv()
     dense = jnp.sum(zx_buf[...], axis=0)
 
     sums = []
     for g in range(3):
-        spread = pltpu.roll(
-            jnp.broadcast_to(dense[g : g + 1], (8, LANES)), 0, 1, stride=NRHS, stride_axis=0
-        )
+        spread = pltpu.roll(jnp.broadcast_to(dense[g : g + 1], (8, LANES)), 0, 1, stride=NRHS, stride_axis=0)
         sums += [spread[(8 - i) % 8 : (8 - i) % 8 + 1] for i in range(8)]
     diag = sums[0:4]
     right = [(sums[4 + k], sums[8 + k]) for k in range(4)]
@@ -309,11 +329,17 @@
     remain = start
     for k in range(4):
         cr, ci = coef[k]
-        term = (cr * basis[k] + ci * times_i(basis[k])) * inverse
+        term = (cr * basis[k] + ci * basis_turned[k]) * inverse
         field = term if field is None else field + term
         remain = remain - cr * images[k] - ci * turned[k]
     x_ref[...] = field
     r_ref[...] = remain
+
+    for k in range(4):
+        halo(k).wait_send()
+    sums_of(0, theta_buf, nz * nx, zx_peers[0]).wait_send()
+    sums_of(1, t_buf, nt, t_peers[0]).wait_send()
+    sums_of(2, zx_buf, nz * nx, zx_peers[0]).wait_send()
 
 
 def prolong_kernel(x_ref, r_ref, nv_ref, out_ref, remain_ref, rows_v):
@@ -342,6 +368,7 @@
     any_spec = pl.BlockSpec(memory_space=pltpu.HBM)
     vmem_spec = pl.BlockSpec(memory_space=pltpu.VMEM)
     field = jax.ShapeDtypeStruct((CDOF, LANES), F32)
+    far = [pltpu.with_memory_space_constraint(a, pltpu.HBM) for a in (res, nv, coarse_op)]
     x, r = pl.pallas_call(
         functools.partial(coarse_kernel, sizes),
         out_shape=(field, field),
@@ -366,7 +393,7 @@
         compiler_params=pltpu.CompilerParams(
             collective_id=0, has_side_effects=True, vmem_limit_bytes=16 * 1024 * 1024
         ),
-    )(res, nv, coarse_op)
+    )(*far)
     correction, remain = pl.pallas_call(
         prolong_kernel,
         out_shape=(

time: 50.4 us -> 44.9 us (0.89)
  local copies, waits for them, and re-layouts: 4.06 us -> 0.01 us
  Pallas kernels: 45.4 us -> 44.1 us
    unnamed x8 -> x2, local copies, waits for them, and re-layouts: 4.06 us -> 0.01 us
    pallas_call x1, Pallas kernels: 44.2 us -> 42.9 us  [body(): pl.pallas_call(functools.partial(coarse_kernel, sizes), out_shape=(field,...]
where the time goes in v2:
time: 44.9 us; the launch traced here: 44.8 us
  Pallas kernels  44.1 us (98%)
  between operations  0.65 us (1%)
    pallas_call x1, Pallas kernels, body(): pl.pallas_call(functools.partial(coarse_kernel, sizes), out_shape=(field,...  42.9 us
    pallas_call x1, Pallas kernels, body(): pl.pallas_call(prolong_kernel, out_shape=(jax.ShapeDtypeStruct((2, 4, 3,...  1.21 us

profile of v2, /device:TPU:1, one launch (start us, length us, event | category | flops | bytes accessed | tf_op | source)
XLA Modules:
  0.0 44.8 jit_solution(9352385169688956810)
XLA Ops:
  0.6 0.0 copy-start
  0.6 42.9 %shard_map.50 = (f32[48,128]{1,0:T(8,128)S(1)}, f32[48,128]{1,0:T(8,128)S(1)}) custom-call(bf16[2,4,3,16,512]{4,3,2,1,0:T(8,128)(2,1)} %bitcast.16, bf16[2,24,3,4,512]{4,3,2,1,0:T(4,128)(2,1)} %bitcast.14, bf16[16,1,1,9,2,48,48]{6,5,4,3,2,1,0:T(8,128)(2,1)} %op_hbm.1), custom_call_target="tpu_custom_call" | custom-call | tf_op jit(solution)/shard_map/pallas_call | solution.py:372
  43.6 0.0 copy-done
  43.6 1.2 %shard_map.51 = (bf16[2,4,3,16,512]{4,3,2,1,0:T(8,128)(2,1)}, f32[2,16,48]{2,1,0:T(8,128)}) custom-call(f32[48,128]{1,0:T(8,128)S(1)} %get-tuple-element.6.x_ref, f32[48,128]{1,0:T(8,128)S(1)} %get-tuple-element.7.r_ref, bf16[2,24,3,4,512]{4,3,2,1,0:T(4,128)(2,1)S(1)} %bitcast.15), custom_call_target="tpu_custom_call" | custom-call | tf_op jit(solution)/shard_map/pallas_call | solution.py:397
Async XLA Ops:
  0.6 42.9 %copy-start = (bf16[2,24,4,3,1,1,1,512]{7,2,6,5,4,3,1,0:T(4,128)(2,1)S(1)}, bf16[2,24,4,3,1,1,1,512]{7,2,6,5,4,3,1,0:T(4,128)(2,1)}, u32[]{:S(2)}) copy-start(bf16[2,24,4,3,1,1,1,512]{7,2,6,5,4,3,1,0:T(4,128)(2,1)} %param.4) | copy-start | bytes 1769476

commit v3 on v2

--- a/solution.py
+++ b/solution.py
@@ -122,6 +122,20 @@
     return [k + jnp.where(k >= me, 1, 0) for k in range(count - 1)]
 
 
+def rank_of(t, nt):
+    half = nt // 2
+    y = lax.div(t, 2)
+    r = jnp.where(y == 0, 0, jnp.where(y <= half // 2, 2 * y - 1, 2 * (half - y)))
+    return 2 * r + lax.rem(t, 2)
+
+
+def slab_of(rank, nt):
+    half = nt // 2
+    r = lax.div(rank, 2)
+    y = jnp.where(lax.rem(r, 2) == 1, lax.div(r + 1, 2), lax.rem(half - lax.div(r, 2), half))
+    return 2 * y + lax.rem(rank, 2)
+
+
 def send_to_all(me, peers, value, buf, send_sem, recv_sem):
     buf[me] = value
     for peer in peers:
@@ -162,6 +176,7 @@
     halo_recv,
     sum_send,
     sum_recv,
+    peers_in,
 ):
     nt, nz, nx = sizes
     t, z, x = lax.axis_index("ta"), lax.axis_index("gz"), lax.axis_index("gy")
@@ -180,13 +195,21 @@
         (1, (lax.rem(t + nt - 1, nt), z, x)),
         (2, (lax.rem(t + 1, nt), z, x)),
     ]
-    far = [(lax.rem(t + d, nt), z, x) for d in range(2, nt - 1)]
-    far += [
-        (t, lax.rem(z + a, nz), lax.rem(x + b, nx))
-        for a in range(nz)
-        for b in range(nx)
-        if (a, b) not in ((0, 0), (1, 0), (nz - 1, 0), (0, 1), (0, nx - 1))
-    ]
+    my_t, my_zx = rank_of(t, nt), me_zx
+
+    def t_peer(rank):
+        return slab_of(rank, nt), z, x
+
+    def zx_peer(rank):
+        return t, lax.div(rank, nx), lax.rem(rank, nx)
+
+    def signal_peers(semaphore, t_ranks, zx_ranks):
+        for ranks, peer in ((t_ranks, t_peer), (zx_ranks, zx_peer)):
+            def step(rank, carry, peer=peer):
+                pl.semaphore_signal(semaphore, inc=1, device_id=peer(rank), device_id_type=MESH)
+                return carry
+            lax.fori_loop(*ranks, step, 0)
+
     barrier = pltpu.get_barrier_semaphore()
     for load in loads[:2]:
         load.start()
@@ -194,15 +217,14 @@
         pl.semaphore_signal(barrier, inc=1, device_id=peer, device_id_type=MESH)
     for load in loads[2:]:
         load.start()
-    for peer in far:
-        pl.semaphore_signal(barrier, inc=1, device_id=peer, device_id_type=MESH)
-    t_peers = [(k, z, x) for k in others(nt, t)]
-    zx_peers = [(t, lax.div(k, nx), lax.rem(k, nx)) for k in others(nz * nx, me_zx)]
+    signal_peers(barrier, (my_t + 1, nt), (my_zx + 1, nz * nx))
+    t_peers = [t_peer(k) for k in others(nt, my_t)]
+    zx_peers = [zx_peer(k) for k in others(nz * nx, my_zx)]
 
     loads[0].wait()
     loads[1].wait()
     start = restrict(nv_v, res_v, rows_v)
-    pl.semaphore_wait(barrier, len(slots) + len(far))
+    pl.semaphore_wait(barrier, len(slots) + my_t + my_zx)
 
     def send_halo(k, field):
         own = packed(field)
@@ -226,6 +248,7 @@
         return transfers(buf.at[pl.ds(0, count - 1)], peer, sum_send.at[k], sum_recv.at[k])
 
     send_halo(0, start)
+    signal_peers(peers_in, (0, my_t), (0, my_zx))
 
     loads[3].wait()
     eye = lax.broadcasted_iota(jnp.int32, (CDOF, CDOF), 0) == lax.broadcasted_iota(jnp.int32, (CDOF, CDOF), 1)
@@ -240,7 +263,6 @@
     stats = [jnp.where(eye, trace[0], 0.0), jnp.where(eye, trace[1], 0.0), square]
     stats = [jnp.sum(row_sum(value), axis=1, keepdims=True) * scale for value in stats]
     stats = jnp.concatenate([jnp.broadcast_to(value, (1, LANES)) for value in stats], axis=0)
-    send_to_all(me_zx, zx_peers, stats, theta_buf, sum_send.at[0], sum_recv.at[0])
 
     loads[2].wait()
     links = jnp.concatenate(
@@ -256,6 +278,14 @@
         halo(k).wait_recv()
         powers.append(apply_links(links, cells[k].reshape(LINKS * CDOF, LANES)))
         send_halo(k + 1, powers[k + 1])
+        if k == 0:
+            answers = nt - 1 - my_t + nz * nx - 1 - my_zx
+
+            @pl.when(answers > 0)
+            def _():
+                pl.semaphore_wait(peers_in, answers)
+
+            send_to_all(me_zx, zx_peers, stats, theta_buf, sum_send.at[0], sum_recv.at[0])
 
     sums_of(0, theta_buf, nz * nx, zx_peers[0]).wait_recv()
     stats = jnp.sum(theta_buf[...], axis=0)
@@ -389,6 +419,7 @@
             pltpu.SemaphoreType.DMA((4,)),
             pltpu.SemaphoreType.DMA((3,)),
             pltpu.SemaphoreType.DMA((3,)),
+            pltpu.SemaphoreType.REGULAR,
         ],
         compiler_params=pltpu.CompilerParams(
             collective_id=0, has_side_effects=True, vmem_limit_bytes=16 * 1024 * 1024

time: 44.9 us -> 41 us (0.913)
  Pallas kernels: 44.1 us -> 40.3 us
    pallas_call x1, Pallas kernels: 42.9 us -> 39 us  [body(): pl.pallas_call(functools.partial(coarse_kernel, sizes), out_shape=(field,...]
where the time goes in v3:
time: 41 us; the launch traced here: 40.9 us
  Pallas kernels  40.3 us (98%)
  between operations  0.65 us (2%)
    pallas_call x1, Pallas kernels, body(): pl.pallas_call(functools.partial(coarse_kernel, sizes), out_shape=(field,...  39 us
    pallas_call x1, Pallas kernels, body(): pl.pallas_call(prolong_kernel, out_shape=(jax.ShapeDtypeStruct((2, 4, 3,...  1.21 us

profile of v3, /device:TPU:1, one launch (start us, length us, event | category | flops | bytes accessed | tf_op | source)
XLA Modules:
  0.0 40.9 jit_solution(7862140314216807637)
XLA Ops:
  0.6 0.0 copy-start
  0.6 39.0 %shard_map.50 = (f32[48,128]{1,0:T(8,128)S(1)}, f32[48,128]{1,0:T(8,128)S(1)}) custom-call(bf16[2,4,3,16,512]{4,3,2,1,0:T(8,128)(2,1)} %bitcast.16, bf16[2,24,3,4,512]{4,3,2,1,0:T(4,128)(2,1)} %bitcast.14, bf16[16,1,1,9,2,48,48]{6,5,4,3,2,1,0:T(8,128)(2,1)} %op_hbm.1), custom_call_target="tpu_custom_call" | custom-call | tf_op jit(solution)/shard_map/pallas_call | solution.py:402
  39.7 0.0 copy-done
  39.7 1.2 %shard_map.51 = (bf16[2,4,3,16,512]{4,3,2,1,0:T(8,128)(2,1)}, f32[2,16,48]{2,1,0:T(8,128)}) custom-call(f32[48,128]{1,0:T(8,128)S(1)} %get-tuple-element.6.x_ref, f32[48,128]{1,0:T(8,128)S(1)} %get-tuple-element.7.r_ref, bf16[2,24,3,4,512]{4,3,2,1,0:T(4,128)(2,1)S(1)} %bitcast.15), custom_call_target="tpu_custom_call" | custom-call | tf_op jit(solution)/shard_map/pallas_call | solution.py:428
Async XLA Ops:
  0.6 39.1 %copy-start = (bf16[2,24,4,3,1,1,1,512]{7,2,6,5,4,3,1,0:T(4,128)(2,1)S(1)}, bf16[2,24,4,3,1,1,1,512]{7,2,6,5,4,3,1,0:T(4,128)(2,1)}, u32[]{:S(2)}) copy-start(bf16[2,24,4,3,1,1,1,512]{7,2,6,5,4,3,1,0:T(4,128)(2,1)} %param.4) | copy-start | bytes 1769476

commit v4 on v3

--- a/solution.py
+++ b/solution.py
@@ -33,11 +33,14 @@
     return sign_of(field.shape) * pltpu.roll(field, 64, 1)
 
 
-def restrict(nv_ref, res_ref, rows_ref):
+def restrict(loads, nv_ref, res_ref, basis_ref, rows_ref):
     total = None
     for colour in range(3):
-        basis = nv_ref[:, :, colour].reshape(2 * NVEC * 4, 512)
-        source = res_ref[:, :, colour].reshape(2 * 4 * NRHS, 512)
+        for load in loads[colour]:
+            load.wait()
+        basis = nv_ref[colour].reshape(2 * NVEC * 4, 512)
+        basis_ref[colour] = basis
+        source = res_ref[colour].reshape(2 * 4 * NRHS, 512)
         part = lax.dot_general(basis, source, (((1,), (1,)), ((), ())), preferred_element_type=F32)
         total = part if total is None else total + part
     rows_ref[...] = total
@@ -55,16 +58,27 @@
     return jnp.where(group == 0, field, 0.0)
 
 
-def packed(field):
-    high = field.astype(BF16).astype(F32)
-    return (high + pltpu.roll(field - high, 2 * NRHS, 1)).astype(BF16)
-
-
-def apply_links(links, cells):
-    product = jnp.dot(links, cells, preferred_element_type=F32)
-    value = product[:CDOF] + times_i(product[CDOF:])
-    value = value + pltpu.roll(value, LANES - 2 * NRHS, 1)
-    return jnp.where(group_of(value.shape) == 0, value, 0.0)
+def split(wide):
+    group = group_of(wide.shape)
+    high = wide.astype(BF16).astype(F32)
+    return jnp.where(group == 0, high, jnp.where(group == 2, wide - high, 0.0)).astype(BF16)
+
+
+def both_groups(field):
+    return field + pltpu.roll(field, 2 * NRHS, 1)
+
+
+def combine(product):
+    real, imag = product[:CDOF], product[CDOF:]
+    first = group_of(real.shape) == 0
+    back, forth = LANES - 2 * NRHS, 2 * NRHS
+    total = real + jnp.where(first, pltpu.roll(real, back, 1), pltpu.roll(real, forth, 1))
+    cross = pltpu.roll(imag, 64, 1) + jnp.where(first, pltpu.roll(imag, forth, 1), pltpu.roll(imag, back, 1))
+    return total + sign_of(real.shape) * cross
+
+
+def first_group(wide):
+    return jnp.where(group_of(wide.shape) == 0, wide, 0.0)
 
 
 def row_sum(product):
@@ -162,6 +176,7 @@
     op_hbm,
     x_ref,
     r_ref,
+    basis_ref,
     res_v,
     nv_v,
     op_v,
@@ -173,6 +188,7 @@
     zx_buf,
     local_sem,
     halo_send,
+    near_recv,
     halo_recv,
     sum_send,
     sum_recv,
@@ -182,18 +198,21 @@
     t, z, x = lax.axis_index("ta"), lax.axis_index("gz"), lax.axis_index("gy")
     me_zx = z * nx + x
     loads = [
-        pltpu.make_async_copy(nv_hbm, nv_v, local_sem.at[0]),
-        pltpu.make_async_copy(res_hbm, res_v, local_sem.at[1]),
-        pltpu.make_async_copy(op_hbm.at[t, 0, 0], op_v, local_sem.at[2]),
-        pltpu.make_async_copy(op_hbm.at[:, 0, 0, 0], col_v, local_sem.at[3]),
+        (
+            pltpu.make_async_copy(nv_hbm.at[:, :, colour], nv_v.at[colour], local_sem.at[2 * colour]),
+            pltpu.make_async_copy(res_hbm.at[:, :, colour], res_v.at[colour], local_sem.at[2 * colour + 1]),
+        )
+        for colour in range(3)
     ]
+    op_load = pltpu.make_async_copy(op_hbm.at[t, 0, 0], op_v, local_sem.at[6])
+    col_load = pltpu.make_async_copy(op_hbm.at[:, 0, 0, 0], col_v, local_sem.at[7])
     slots = [
-        (3, (t, lax.rem(z + nz - 1, nz), x)),
-        (4, (t, lax.rem(z + 1, nz), x)),
-        (5, (t, z, lax.rem(x + nx - 1, nx))),
-        (6, (t, z, lax.rem(x + 1, nx))),
-        (1, (lax.rem(t + nt - 1, nt), z, x)),
-        (2, (lax.rem(t + 1, nt), z, x)),
+        (5, (t, lax.rem(z + nz - 1, nz), x)),
+        (6, (t, lax.rem(z + 1, nz), x)),
+        (7, (t, z, lax.rem(x + nx - 1, nx))),
+        (8, (t, z, lax.rem(x + 1, nx))),
+        (3, (lax.rem(t + nt - 1, nt), z, x)),
+        (4, (lax.rem(t + 1, nt), z, x)),
     ]
     my_t, my_zx = rank_of(t, nt), me_zx
 
@@ -211,46 +230,49 @@
             lax.fori_loop(*ranks, step, 0)
 
     barrier = pltpu.get_barrier_semaphore()
-    for load in loads[:2]:
-        load.start()
+    for pair in loads:
+        for load in pair:
+            load.start()
     for _, peer in slots:
         pl.semaphore_signal(barrier, inc=1, device_id=peer, device_id_type=MESH)
-    for load in loads[2:]:
-        load.start()
     signal_peers(barrier, (my_t + 1, nt), (my_zx + 1, nz * nx))
     t_peers = [t_peer(k) for k in others(nt, my_t)]
     zx_peers = [zx_peer(k) for k in others(nz * nx, my_zx)]
 
-    loads[0].wait()
-    loads[1].wait()
-    start = restrict(nv_v, res_v, rows_v)
+    op_load.start()
+    col_load.start()
+    start = restrict(loads, nv_v, res_v, basis_ref, rows_v)
     pl.semaphore_wait(barrier, len(slots) + my_t + my_zx)
 
-    def send_halo(k, field):
-        own = packed(field)
+    def send_halo(k, wide):
+        own = split(wide)
         cells[k, 0] = own
         for m, peer in slots:
             pltpu.make_async_remote_copy(
                 src_ref=cells.at[k, 0],
                 dst_ref=cells.at[k, m],
                 send_sem=halo_send.at[k],
-                recv_sem=halo_recv.at[k],
+                recv_sem=(near_recv if m < 5 else halo_recv).at[k],
                 device_id=peer,
                 device_id_type=MESH,
             ).start()
-        cells[k, 7] = own
-        cells[k, 8] = own
-
-    def halo(k):
-        return transfers(cells.at[k, pl.ds(1, 6)], slots[0][1], halo_send.at[k], halo_recv.at[k])
+        cells[k, 1] = own
+        cells[k, 2] = own
+
+    def apply_links(k):
+        transfers(cells.at[k, pl.ds(3, 2)], slots[0][1], halo_send.at[k], near_recv.at[k]).wait_recv()
+        near = jnp.dot(links[0], cells[k, 0:5].reshape(5 * CDOF, LANES), preferred_element_type=F32)
+        transfers(cells.at[k, pl.ds(5, 4)], slots[0][1], halo_send.at[k], halo_recv.at[k]).wait_recv()
+        far = jnp.dot(links[1], cells[k, 5:9].reshape(4 * CDOF, LANES), preferred_element_type=F32)
+        return combine(near + far)
 
     def sums_of(k, buf, count, peer):
         return transfers(buf.at[pl.ds(0, count - 1)], peer, sum_send.at[k], sum_recv.at[k])
 
-    send_halo(0, start)
+    send_halo(0, both_groups(start))
     signal_peers(peers_in, (0, my_t), (0, my_zx))
 
-    loads[3].wait()
+    col_load.wait()
     eye = lax.broadcasted_iota(jnp.int32, (CDOF, CDOF), 0) == lax.broadcasted_iota(jnp.int32, (CDOF, CDOF), 1)
     trace = [jnp.zeros((CDOF, CDOF), F32), jnp.zeros((CDOF, CDOF), F32)]
     square = jnp.zeros((CDOF, CDOF), F32)
@@ -264,20 +286,19 @@
     stats = [jnp.sum(row_sum(value), axis=1, keepdims=True) * scale for value in stats]
     stats = jnp.concatenate([jnp.broadcast_to(value, (1, LANES)) for value in stats], axis=0)
 
-    loads[2].wait()
-    links = jnp.concatenate(
-        [
-            jnp.concatenate([op_v[m, part].astype(F32) for m in range(LINKS)], axis=1)
-            for part in range(2)
-        ],
-        axis=0,
-    ).astype(BF16)
+    op_load.wait()
+    links = [
+        jnp.concatenate(
+            [jnp.concatenate([op_v[m, part].astype(F32) for m in order], axis=1) for part in range(2)], axis=0
+        ).astype(BF16)
+        for order in ((0, 7, 8, 1, 2), (3, 4, 5, 6))
+    ]
 
     powers = [start]
     for k in range(3):
-        halo(k).wait_recv()
-        powers.append(apply_links(links, cells[k].reshape(LINKS * CDOF, LANES)))
-        send_halo(k + 1, powers[k + 1])
+        wide = apply_links(k)
+        send_halo(k + 1, wide)
+        powers.append(first_group(wide))
         if k == 0:
             answers = nt - 1 - my_t + nz * nx - 1 - my_zx
 
@@ -309,33 +330,31 @@
     turned = [times_i(image) for image in images]
     start_turned = times_i(start)
 
-    pairs = [(i, j) for j in range(4) for i in range(j)]
-    norms = [row_sum(images[k] * images[k]) for k in range(3)]
-    right = [row_sum(images[k] * start) for k in range(3)]
-    right_i = [row_sum(turned[k] * start) for k in range(3)]
-    cross = [row_sum(images[i] * images[j]) for i, j in pairs[:3]]
-    cross_i = [row_sum(turned[i] * images[j]) for i, j in pairs[:3]]
-
-    halo(3).wait_recv()
-    newest = apply_links(links, cells[3].reshape(LINKS * CDOF, LANES)) * weights[3]
+    def row_of(rows, first):
+        table = jnp.concatenate(rows, axis=0)
+        table = table + pltpu.roll(table, 64, 1)
+        table = jnp.where(lane_iota(table.shape) < NRHS, table, 0.0)
+        return row_sum(pltpu.roll(table, first * NRHS, 1, stride=NRHS, stride_axis=0))
+
+    early_pairs, late_pairs = [(0, 1), (0, 2), (1, 2)], [(0, 3), (1, 3), (2, 3)]
+    early = [row_sum(images[k] * images[k]) for k in range(3)]
+    early += [row_sum(images[k] * start) for k in range(3)]
+    early += [row_sum(turned[k] * start) for k in range(3)]
+    early += [row_sum(images[i] * images[j]) for i, j in early_pairs]
+    early += [row_sum(turned[i] * images[j]) for i, j in early_pairs]
+    early = [row_of(early[:8], 0), row_of(early[8:15] + [jnp.zeros((1, LANES), F32)], 0)]
+
+    newest = first_group(apply_links(3)) * weights[3]
     for part in last:
         newest = newest - part
     images.append(newest + last[3])
-    norms.append(row_sum(images[3] * images[3]))
-    right.append(row_sum(images[3] * start))
-    right_i.append(-row_sum(images[3] * start_turned))
-    cross += [row_sum(images[i] * images[3]) for i in range(3)]
-    cross_i += [row_sum(turned[i] * images[3]) for i in range(3)]
-    table = jnp.concatenate(norms + right + right_i + cross + cross_i, axis=0)
-    table = table + pltpu.roll(table, 64, 1)
-    table = jnp.where(lane_iota(table.shape) < NRHS, table, 0.0)
-    dense = jnp.concatenate(
-        [
-            row_sum(pltpu.roll(table[8 * g : 8 * g + 8], 0, 1, stride=NRHS, stride_axis=0))
-            for g in range(3)
-        ],
-        axis=0,
-    )
+    late = [row_sum(images[3] * images[3]), row_sum(images[3] * start), -row_sum(images[3] * start_turned)]
+    late += [row_sum(images[i] * images[3]) for i in range(3)]
+    late += [row_sum(turned[i] * images[3]) for i in range(3)]
+    seven = jnp.concatenate([late[0], jnp.zeros((7, LANES), F32)], axis=0)
+    seven = seven + pltpu.roll(seven, 64, 1)
+    seven = pltpu.roll(jnp.where(lane_iota(seven.shape) < NRHS, seven, 0.0), 7 * NRHS, 1)[0:1]
+    dense = jnp.concatenate([early[0], early[1] + seven, row_of(late[1:], 0)], axis=0)
 
     send_to_all(t, t_peers, dense, t_buf, sum_send.at[1], sum_recv.at[1])
     turned.append(times_i(images[3]))
@@ -350,9 +369,10 @@
     for g in range(3):
         spread = pltpu.roll(jnp.broadcast_to(dense[g : g + 1], (8, LANES)), 0, 1, stride=NRHS, stride_axis=0)
         sums += [spread[(8 - i) % 8 : (8 - i) % 8 + 1] for i in range(8)]
-    diag = sums[0:4]
-    right = [(sums[4 + k], sums[8 + k]) for k in range(4)]
-    upper = {pair: (sums[12 + n], sums[18 + n]) for n, pair in enumerate(pairs)}
+    diag = sums[0:3] + [sums[15]]
+    right = [(sums[3 + k], sums[6 + k]) for k in range(3)] + [(sums[16], sums[17])]
+    upper = {pair: (sums[9 + n], sums[12 + n]) for n, pair in enumerate(early_pairs)}
+    upper.update({pair: (sums[18 + n], sums[21 + n]) for n, pair in enumerate(late_pairs)})
     coef = [(both_halves(c[0]), both_halves(c[1])) for c in solve(diag, upper, right)]
 
     field = None
@@ -366,13 +386,13 @@
     r_ref[...] = remain
 
     for k in range(4):
-        halo(k).wait_send()
+        transfers(cells.at[k, pl.ds(3, 6)], slots[0][1], halo_send.at[k], halo_recv.at[k]).wait_send()
     sums_of(0, theta_buf, nz * nx, zx_peers[0]).wait_send()
     sums_of(1, t_buf, nt, t_peers[0]).wait_send()
     sums_of(2, zx_buf, nz * nx, zx_peers[0]).wait_send()
 
 
-def prolong_kernel(x_ref, r_ref, nv_ref, out_ref, remain_ref, rows_v):
+def prolong_kernel(x_ref, r_ref, basis_ref, out_ref, remain_ref, rows_v):
     x = x_ref[...].astype(BF16).astype(F32)
     upper, lower = x[:NVEC], x[NVEC:]
     every = upper + pltpu.roll(upper, NRHS, 1) + pltpu.roll(lower, 2 * NRHS, 1) + pltpu.roll(lower, 3 * NRHS, 1)
@@ -382,8 +402,7 @@
         rows_v[pl.ds(s, 2 * NVEC, stride=4), :] = jnp.where(group == s, every, 0.0)
     weights = rows_v[...].T.astype(BF16)
     for colour in range(3):
-        basis = nv_ref[:, :, colour].reshape(2 * NVEC * 4, 512)
-        value = jnp.dot(weights, basis, preferred_element_type=F32)
+        value = jnp.dot(weights, basis_ref[colour], preferred_element_type=F32)
         out_ref[:, :, colour] = value.astype(BF16).reshape(2, 4, NRHS, 512)
     turned = r_ref[...].T
     remain_ref[0] = turned[0:NRHS]
@@ -399,14 +418,14 @@
     vmem_spec = pl.BlockSpec(memory_space=pltpu.VMEM)
     field = jax.ShapeDtypeStruct((CDOF, LANES), F32)
     far = [pltpu.with_memory_space_constraint(a, pltpu.HBM) for a in (res, nv, coarse_op)]
-    x, r = pl.pallas_call(
+    x, r, basis = pl.pallas_call(
         functools.partial(coarse_kernel, sizes),
-        out_shape=(field, field),
+        out_shape=(field, field, jax.ShapeDtypeStruct((3, 2 * NVEC * 4, sites), BF16)),
         in_specs=[any_spec] * 3,
-        out_specs=(vmem_spec, vmem_spec),
+        out_specs=(vmem_spec,) * 3,
         scratch_shapes=[
-            pltpu.VMEM(res.shape, BF16),
-            pltpu.VMEM(nv.shape, BF16),
+            pltpu.VMEM((3, 2, 4, NRHS, sites), BF16),
+            pltpu.VMEM((3, 2, NVEC, 4, sites), BF16),
             pltpu.VMEM((LINKS, 2, CDOF, CDOF), BF16),
             pltpu.VMEM((nt, 2, CDOF, CDOF), BF16),
             pltpu.VMEM((2 * NVEC * 4, LANES), F32),
@@ -414,6 +433,7 @@
             pltpu.VMEM((nz * nx, 3, LANES), F32),
             pltpu.VMEM((nt, 3, LANES), F32),
             pltpu.VMEM((nz * nx, 3, LANES), F32),
+            pltpu.SemaphoreType.DMA((8,)),
             pltpu.SemaphoreType.DMA((4,)),
             pltpu.SemaphoreType.DMA((4,)),
             pltpu.SemaphoreType.DMA((4,)),
@@ -435,7 +455,7 @@
         out_specs=(vmem_spec, vmem_spec),
         scratch_shapes=[pltpu.VMEM((2 * NVEC * 4, LANES), F32)],
         compiler_params=pltpu.CompilerParams(vmem_limit_bytes=16 * 1024 * 1024),
-    )(x, r, nv)
+    )(x, r, basis)
     correction = correction.reshape(2, 4, 3, NRHS, 1, 1, 1, sites)
     remain = remain.transpose(0, 2, 1).reshape(2, CDOF, 1, 1, 1, NRHS)
     return correction, remain

time: 41 us -> 40.5 us (0.988)
  Pallas kernels: 40.3 us -> 39.8 us
    pallas_call x1, Pallas kernels: 39 us -> 38.6 us  [body(): pl.pallas_call(functools.partial(coarse_kernel, sizes), out_shape=(field,...]
where the time goes in v4:
time: 40.5 us; the launch traced here: 40.4 us
  Pallas kernels  39.8 us (98%)
  between operations  0.64 us (2%)
    pallas_call x1, Pallas kernels, body(): pl.pallas_call(functools.partial(coarse_kernel, sizes), out_shape=(field,...  38.6 us
    pallas_call x1, Pallas kernels, body(): pl.pallas_call(prolong_kernel, out_shape=(jax.ShapeDtypeStruct((2, 4, 3,...  1.21 us

profile of v4, /device:TPU:1, one launch (start us, length us, event | category | flops | bytes accessed | tf_op | source)
XLA Modules:
  0.0 40.4 jit_solution(1291015858841182034)
XLA Ops:
  0.6 38.6 %shard_map.50 = (f32[48,128]{1,0:T(8,128)S(1)}, f32[48,128]{1,0:T(8,128)S(1)}, bf16[3,192,512]{2,1,0:T(8,128)(2,1)S(1)}) custom-call(bf16[2,4,3,16,512]{4,3,2,1,0:T(8,128)(2,1)} %bitcast.15, bf16[2,24,3,4,512]{4,3,2,1,0:T(4,128)(2,1)} %bitcast.14, bf16[16,1,1,9,2,48,48]{6,5,4,3,2,1,0:T(8,128)(2,1)} %op_hbm.1), custom_call_target="tpu_custom_call" | custom-call | tf_op jit(solution)/shard_map/pallas_call | solution.py:421
  39.2 1.2 %shard_map.51 = (bf16[2,4,3,16,512]{4,3,2,1,0:T(8,128)(2,1)}, f32[2,16,48]{2,1,0:T(8,128)}) custom-call(f32[48,128]{1,0:T(8,128)S(1)} %get-tuple-element.7.x_ref, f32[48,128]{1,0:T(8,128)S(1)} %get-tuple-element.8.r_ref, bf16[3,192,512]{2,1,0:T(8,128)(2,1)S(1)} %get-tuple-element.9.basis_ref), custom_call_target="tpu_custom_call" | custom-call | tf_op jit(solution)/shard_map/pallas_call | solution.py:448

commit v5 on v4

--- a/solution.py
+++ b/solution.py
@@ -150,6 +150,35 @@
     return 2 * y + lax.rem(rank, 2)
 
 
+def ball(sizes):
+    steps = [(1, 0, 0), (-1, 0, 0), (0, 1, 0), (0, -1, 0), (0, 0, 1), (0, 0, -1)]
+    found = [(0, 0, 0)] + [shifted((0, 0, 0), step, sizes) for step in steps]
+    for a in steps:
+        for b in steps:
+            site = shifted(shifted((0, 0, 0), a, sizes), b, sizes)
+            if site not in found:
+                found.append(site)
+    return steps, found
+
+
+def shifted(site, step, sizes):
+    return tuple((a + b) % n for a, b, n in zip(site, step, sizes))
+
+
+def pack_links(op_ref):
+    def rows(part):
+        near = [op_ref[m, part].astype(F32) for m in (0, 7, 8, 1, 2)]
+        far = [op_ref[m, part].astype(F32) for m in (3, 4, 5, 6)]
+        return jnp.concatenate(near + [jnp.zeros((CDOF, 16), F32)] + far + [jnp.zeros((CDOF, 64), F32)], axis=1)
+
+    return jnp.concatenate([rows(0), rows(1)], axis=0).astype(BF16)
+
+
+def times_links(links, near, far):
+    value = jnp.dot(links[:, : 5 * CDOF], near, preferred_element_type=F32)
+    return combine(value + jnp.dot(links[:, 256 : 256 + 4 * CDOF], far, preferred_element_type=F32))
+
+
 def send_to_all(me, peers, value, buf, send_sem, recv_sem):
     buf[me] = value
     for peer in peers:
@@ -183,6 +212,8 @@
     col_v,
     rows_v,
     cells,
+    links_v,
+    ball_v,
     theta_buf,
     t_buf,
     zx_buf,
@@ -193,6 +224,10 @@
     sum_send,
     sum_recv,
     peers_in,
+    links_send,
+    links_recv,
+    ball_send,
+    ball_recv,
 ):
     nt, nz, nx = sizes
     t, z, x = lax.axis_index("ta"), lax.axis_index("gz"), lax.axis_index("gy")
@@ -204,8 +239,15 @@
         )
         for colour in range(3)
     ]
-    op_load = pltpu.make_async_copy(op_hbm.at[t, 0, 0], op_v, local_sem.at[6])
-    col_load = pltpu.make_async_copy(op_hbm.at[:, 0, 0, 0], col_v, local_sem.at[7])
+    op_loads = [
+        pltpu.make_async_copy(op_hbm.at[slab, 0, 0], op_v.at[i], local_sem.at[6 + i])
+        for i, slab in enumerate((t, lax.rem(t + 1, nt), lax.rem(t + nt - 1, nt)))
+    ]
+    col_load = pltpu.make_async_copy(op_hbm.at[:, 0, 0, 0], col_v, local_sem.at[9])
+    steps, sites = ball(sizes)
+    ball_peers = [
+        (lax.rem(t + nt - a, nt), lax.rem(z + nz - b, nz), lax.rem(x + nx - c, nx)) for a, b, c in sites
+    ]
     slots = [
         (5, (t, lax.rem(z + nz - 1, nz), x)),
         (6, (t, lax.rem(z + 1, nz), x)),
@@ -233,16 +275,17 @@
     for pair in loads:
         for load in pair:
             load.start()
-    for _, peer in slots:
+    for peer in ball_peers[1:]:
         pl.semaphore_signal(barrier, inc=1, device_id=peer, device_id_type=MESH)
     signal_peers(barrier, (my_t + 1, nt), (my_zx + 1, nz * nx))
     t_peers = [t_peer(k) for k in others(nt, my_t)]
     zx_peers = [zx_peer(k) for k in others(nz * nx, my_zx)]
 
-    op_load.start()
+    for load in op_loads:
+        load.start()
     col_load.start()
     start = restrict(loads, nv_v, res_v, basis_ref, rows_v)
-    pl.semaphore_wait(barrier, len(slots) + my_t + my_zx)
+    pl.semaphore_wait(barrier, len(sites) - 1 + my_t + my_zx)
 
     def send_halo(k, wide):
         own = split(wide)
@@ -261,9 +304,13 @@
 
     def apply_links(k):
         transfers(cells.at[k, pl.ds(3, 2)], slots[0][1], halo_send.at[k], near_recv.at[k]).wait_recv()
-        near = jnp.dot(links[0], cells[k, 0:5].reshape(5 * CDOF, LANES), preferred_element_type=F32)
+        near = jnp.dot(
+            links_v[0, :, : 5 * CDOF], cells[k, 0:5].reshape(5 * CDOF, LANES), preferred_element_type=F32
+        )
         transfers(cells.at[k, pl.ds(5, 4)], slots[0][1], halo_send.at[k], halo_recv.at[k]).wait_recv()
-        far = jnp.dot(links[1], cells[k, 5:9].reshape(4 * CDOF, LANES), preferred_element_type=F32)
+        far = jnp.dot(
+            links_v[0, :, 256 : 256 + 4 * CDOF], cells[k, 5:9].reshape(4 * CDOF, LANES), preferred_element_type=F32
+        )
         return combine(near + far)
 
     def sums_of(k, buf, count, peer):
@@ -271,6 +318,18 @@
 
     send_halo(0, both_groups(start))
     signal_peers(peers_in, (0, my_t), (0, my_zx))
+
+    op_loads[0].wait()
+    links_v[0] = pack_links(op_v.at[0])
+    for i in range(3, 7):
+        pltpu.make_async_remote_copy(
+            src_ref=links_v.at[0],
+            dst_ref=links_v.at[i],
+            send_sem=links_send,
+            recv_sem=links_recv,
+            device_id=ball_peers[i],
+            device_id_type=MESH,
+        ).start()
 
     col_load.wait()
     eye = lax.broadcasted_iota(jnp.int32, (CDOF, CDOF), 0) == lax.broadcasted_iota(jnp.int32, (CDOF, CDOF), 1)
@@ -286,27 +345,33 @@
     stats = [jnp.sum(row_sum(value), axis=1, keepdims=True) * scale for value in stats]
     stats = jnp.concatenate([jnp.broadcast_to(value, (1, LANES)) for value in stats], axis=0)
 
-    op_load.wait()
-    links = [
-        jnp.concatenate(
-            [jnp.concatenate([op_v[m, part].astype(F32) for m in order], axis=1) for part in range(2)], axis=0
-        ).astype(BF16)
-        for order in ((0, 7, 8, 1, 2), (3, 4, 5, 6))
-    ]
+    for i in (1, 2):
+        op_loads[i].wait()
+        links_v[i] = pack_links(op_v.at[i])
 
     powers = [start]
-    for k in range(3):
-        wide = apply_links(k)
-        send_halo(k + 1, wide)
-        powers.append(first_group(wide))
-        if k == 0:
-            answers = nt - 1 - my_t + nz * nx - 1 - my_zx
-
-            @pl.when(answers > 0)
-            def _():
-                pl.semaphore_wait(peers_in, answers)
-
-            send_to_all(me_zx, zx_peers, stats, theta_buf, sum_send.at[0], sum_recv.at[0])
+    wide = apply_links(0)
+    send_halo(1, wide)
+    powers.append(first_group(wide))
+    answers = nt - 1 - my_t + nz * nx - 1 - my_zx
+
+    @pl.when(answers > 0)
+    def _():
+        pl.semaphore_wait(peers_in, answers)
+
+    send_to_all(me_zx, zx_peers, stats, theta_buf, sum_send.at[0], sum_recv.at[0])
+    wide = apply_links(1)
+    ball_v[0] = split(wide)
+    for i in reversed(range(1, len(sites))):
+        pltpu.make_async_remote_copy(
+            src_ref=ball_v.at[0],
+            dst_ref=ball_v.at[i],
+            send_sem=ball_send,
+            recv_sem=ball_recv,
+            device_id=ball_peers[i],
+            device_id_type=MESH,
+        ).start()
+    powers.append(first_group(wide))
 
     sums_of(0, theta_buf, nz * nx, zx_peers[0]).wait_recv()
     stats = jnp.sum(theta_buf[...], axis=0)
@@ -320,15 +385,14 @@
     def times_theta(field):
         return theta[0] * field + theta[1] * times_i(field)
 
-    level = [start] + [powers[k] * weights[k - 1] for k in range(1, 4)]
-    basis, last = [start], [times_theta(level[3])]
-    for _ in range(3):
-        level = [level[i + 1] - times_theta(level[i]) for i in range(len(level) - 1)]
-        basis.append(level[0])
-        last.append(times_theta(level[-1]))
-    images = [basis[k + 1] + times_theta(basis[k]) for k in range(3)]
+    v1, v2 = powers[1] * weights[0], powers[2] * weights[1]
+    one = [v1 - times_theta(start), v2 - times_theta(v1)]
+    two = one[1] - times_theta(one[0])
+    basis = [start, one[0], two]
+    images = [v1, two + times_theta(one[0])]
     turned = [times_i(image) for image in images]
     start_turned = times_i(start)
+    last_one, last_two, last_three = times_theta(v2), times_theta(one[1]), times_theta(two)
 
     def row_of(rows, first):
         table = jnp.concatenate(rows, axis=0)
@@ -336,25 +400,44 @@
         table = jnp.where(lane_iota(table.shape) < NRHS, table, 0.0)
         return row_sum(pltpu.roll(table, first * NRHS, 1, stride=NRHS, stride_axis=0))
 
-    early_pairs, late_pairs = [(0, 1), (0, 2), (1, 2)], [(0, 3), (1, 3), (2, 3)]
-    early = [row_sum(images[k] * images[k]) for k in range(3)]
-    early += [row_sum(images[k] * start) for k in range(3)]
-    early += [row_sum(turned[k] * start) for k in range(3)]
-    early += [row_sum(images[i] * images[j]) for i, j in early_pairs]
-    early += [row_sum(turned[i] * images[j]) for i, j in early_pairs]
-    early = [row_of(early[:8], 0), row_of(early[8:15] + [jnp.zeros((1, LANES), F32)], 0)]
-
-    newest = first_group(apply_links(3)) * weights[3]
-    for part in last:
-        newest = newest - part
-    images.append(newest + last[3])
-    late = [row_sum(images[3] * images[3]), row_sum(images[3] * start), -row_sum(images[3] * start_turned)]
-    late += [row_sum(images[i] * images[3]) for i in range(3)]
-    late += [row_sum(turned[i] * images[3]) for i in range(3)]
-    seven = jnp.concatenate([late[0], jnp.zeros((7, LANES), F32)], axis=0)
-    seven = seven + pltpu.roll(seven, 64, 1)
-    seven = pltpu.roll(jnp.where(lane_iota(seven.shape) < NRHS, seven, 0.0), 7 * NRHS, 1)[0:1]
-    dense = jnp.concatenate([early[0], early[1] + seven, row_of(late[1:], 0)], axis=0)
+    early = [row_sum(images[k] * images[k]) for k in range(2)]
+    early += [row_sum(images[k] * start) for k in range(2)]
+    early += [row_sum(turned[k] * start) for k in range(2)]
+    early += [row_sum(images[0] * images[1]), row_sum(turned[0] * images[1])]
+    early = row_of(early, 0)
+
+    transfers(links_v.at[pl.ds(3, 4)], ball_peers[1], links_send, links_recv).wait_recv()
+    transfers(ball_v.at[pl.ds(1, len(sites) - 1)], ball_peers[1], ball_send, ball_recv).wait_recv()
+
+    def block(site, step=(0, 0, 0)):
+        return ball_v[sites.index(shifted(site, step, sizes))]
+
+    parts = []
+    for i in range(7):
+        own = block(sites[i])
+        near = jnp.concatenate([own] * 3 + [block(sites[i], step) for step in steps[:2]], axis=0)
+        far = jnp.concatenate([block(sites[i], step) for step in steps[2:]], axis=0)
+        wide = times_links(links_v[i], near, far)
+        parts.append(split(wide))
+        if i == 0:
+            v3 = first_group(wide) * weights[2]
+    near = jnp.concatenate([parts[0]] * 3 + parts[1:3], axis=0)
+    v4 = first_group(times_links(links_v[0], near, jnp.concatenate(parts[3:], axis=0))) * weights[3]
+
+    one.append(v3 - last_one)
+    two_next = one[2] - last_two
+    basis.append(two_next - last_three)
+    images.append(basis[3] + last_three)
+    turned.append(times_i(images[2]))
+    images.append(v4 - times_theta(v3) - times_theta(one[2]) - times_theta(two_next))
+    late = [row_sum(images[k] * images[k]) for k in (2, 3)]
+    late += [row_sum(images[k] * start) for k in (2, 3)]
+    late += [row_sum(turned[2] * start), -row_sum(images[3] * start_turned)]
+    late += [row_sum(images[i] * images[2]) for i in (0, 1)]
+    late += [row_sum(images[i] * images[3]) for i in (0, 1, 2)]
+    late += [row_sum(turned[i] * images[2]) for i in (0, 1)]
+    late += [row_sum(turned[i] * images[3]) for i in (0, 1, 2)]
+    dense = jnp.concatenate([early, row_of(late[:8], 0), row_of(late[8:], 0)], axis=0)
 
     send_to_all(t, t_peers, dense, t_buf, sum_send.at[1], sum_recv.at[1])
     turned.append(times_i(images[3]))
@@ -369,10 +452,16 @@
     for g in range(3):
         spread = pltpu.roll(jnp.broadcast_to(dense[g : g + 1], (8, LANES)), 0, 1, stride=NRHS, stride_axis=0)
         sums += [spread[(8 - i) % 8 : (8 - i) % 8 + 1] for i in range(8)]
-    diag = sums[0:3] + [sums[15]]
-    right = [(sums[3 + k], sums[6 + k]) for k in range(3)] + [(sums[16], sums[17])]
-    upper = {pair: (sums[9 + n], sums[12 + n]) for n, pair in enumerate(early_pairs)}
-    upper.update({pair: (sums[18 + n], sums[21 + n]) for n, pair in enumerate(late_pairs)})
+    diag = sums[0:2] + sums[8:10]
+    right = [(sums[2], sums[4]), (sums[3], sums[5]), (sums[10], sums[12]), (sums[11], sums[13])]
+    upper = {
+        (0, 1): (sums[6], sums[7]),
+        (0, 2): (sums[14], sums[19]),
+        (1, 2): (sums[15], sums[20]),
+        (0, 3): (sums[16], sums[21]),
+        (1, 3): (sums[17], sums[22]),
+        (2, 3): (sums[18], sums[23]),
+    }
     coef = [(both_halves(c[0]), both_halves(c[1])) for c in solve(diag, upper, right)]
 
     field = None
@@ -385,7 +474,9 @@
     x_ref[...] = field
     r_ref[...] = remain
 
-    for k in range(4):
+    transfers(links_v.at[pl.ds(3, 4)], ball_peers[1], links_send, links_recv).wait_send()
+    transfers(ball_v.at[pl.ds(1, len(sites) - 1)], ball_peers[1], ball_send, ball_recv).wait_send()
+    for k in range(2):
         transfers(cells.at[k, pl.ds(3, 6)], slots[0][1], halo_send.at[k], halo_recv.at[k]).wait_send()
     sums_of(0, theta_buf, nz * nx, zx_peers[0]).wait_send()
     sums_of(1, t_buf, nt, t_peers[0]).wait_send()
@@ -426,20 +517,26 @@
         scratch_shapes=[
             pltpu.VMEM((3, 2, 4, NRHS, sites), BF16),
             pltpu.VMEM((3, 2, NVEC, 4, sites), BF16),
-            pltpu.VMEM((LINKS, 2, CDOF, CDOF), BF16),
+            pltpu.VMEM((3, LINKS, 2, CDOF, CDOF), BF16),
             pltpu.VMEM((nt, 2, CDOF, CDOF), BF16),
             pltpu.VMEM((2 * NVEC * 4, LANES), F32),
-            pltpu.VMEM((4, LINKS, CDOF, LANES), BF16),
+            pltpu.VMEM((2, LINKS, CDOF, LANES), BF16),
+            pltpu.VMEM((7, 2 * CDOF, 512), BF16),
+            pltpu.VMEM((len(ball(sizes)[1]), CDOF, LANES), BF16),
             pltpu.VMEM((nz * nx, 3, LANES), F32),
             pltpu.VMEM((nt, 3, LANES), F32),
             pltpu.VMEM((nz * nx, 3, LANES), F32),
-            pltpu.SemaphoreType.DMA((8,)),
-            pltpu.SemaphoreType.DMA((4,)),
-            pltpu.SemaphoreType.DMA((4,)),
-            pltpu.SemaphoreType.DMA((4,)),
+            pltpu.SemaphoreType.DMA((10,)),
+            pltpu.SemaphoreType.DMA((2,)),
+            pltpu.SemaphoreType.DMA((2,)),
+            pltpu.SemaphoreType.DMA((2,)),
             pltpu.SemaphoreType.DMA((3,)),
             pltpu.SemaphoreType.DMA((3,)),
             pltpu.SemaphoreType.REGULAR,
+            pltpu.SemaphoreType.DMA,
+            pltpu.SemaphoreType.DMA,
+            pltpu.SemaphoreType.DMA,
+            pltpu.SemaphoreType.DMA,
         ],
         compiler_params=pltpu.CompilerParams(
             collective_id=0, has_side_effects=True, vmem_limit_bytes=16 * 1024 * 1024

time: 40.5 us -> 39.7 us (0.980)
  Pallas kernels: 39.8 us -> 38.9 us
    pallas_call x1, Pallas kernels: 38.6 us -> 37.7 us  [body(): pl.pallas_call(functools.partial(coarse_kernel, sizes), out_shape=(field,...]
where the time goes in v5:
time: 39.7 us; the launch traced here: 39.6 us
  Pallas kernels  38.9 us (98%)
  between operations  0.64 us (2%)
    pallas_call x1, Pallas kernels, body(): pl.pallas_call(functools.partial(coarse_kernel, sizes), out_shape=(field,...  37.7 us
    pallas_call x1, Pallas kernels, body(): pl.pallas_call(prolong_kernel, out_shape=(jax.ShapeDtypeStruct((2, 4, 3,...  1.21 us

profile of v5, /device:TPU:1, one launch (start us, length us, event | category | flops | bytes accessed | tf_op | source)
XLA Modules:
  0.0 39.6 jit_solution(8363388708706462175)
XLA Ops:
  0.6 37.7 %shard_map.50 = (f32[48,128]{1,0:T(8,128)S(1)}, f32[48,128]{1,0:T(8,128)S(1)}, bf16[3,192,512]{2,1,0:T(8,128)(2,1)S(1)}) custom-call(bf16[2,4,3,16,512]{4,3,2,1,0:T(8,128)(2,1)} %bitcast.15, bf16[2,24,3,4,512]{4,3,2,1,0:T(4,128)(2,1)} %bitcast.14, bf16[16,1,1,9,2,48,48]{6,5,4,3,2,1,0:T(8,128)(2,1)} %op_hbm.1), custom_call_target="tpu_custom_call" | custom-call | tf_op jit(solution)/shard_map/pallas_call | solution.py:512
  38.4 1.2 %shard_map.51 = (bf16[2,4,3,16,512]{4,3,2,1,0:T(8,128)(2,1)}, f32[2,16,48]{2,1,0:T(8,128)}) custom-call(f32[48,128]{1,0:T(8,128)S(1)} %get-tuple-element.7.x_ref, f32[48,128]{1,0:T(8,128)S(1)} %get-tuple-element.8.r_ref, bf16[3,192,512]{2,1,0:T(8,128)(2,1)S(1)} %get-tuple-element.9.basis_ref), custom_call_target="tpu_custom_call" | custom-call | tf_op jit(solution)/shard_map/pallas_call | solution.py:545

commit v6 on v5

--- a/solution.py
+++ b/solution.py
@@ -167,16 +167,17 @@
 
 def pack_links(op_ref):
     def rows(part):
-        near = [op_ref[m, part].astype(F32) for m in (0, 7, 8, 1, 2)]
-        far = [op_ref[m, part].astype(F32) for m in (3, 4, 5, 6)]
-        return jnp.concatenate(near + [jnp.zeros((CDOF, 16), F32)] + far + [jnp.zeros((CDOF, 64), F32)], axis=1)
+        blocks = [op_ref[m, part].astype(F32) for m in range(LINKS)]
+        own = blocks[0] + (blocks[7] + blocks[8])
+        high = own.astype(BF16).astype(F32)
+        return jnp.concatenate([high, own - high] + blocks[1:7], axis=1)
 
     return jnp.concatenate([rows(0), rows(1)], axis=0).astype(BF16)
 
 
-def times_links(links, near, far):
-    value = jnp.dot(links[:, : 5 * CDOF], near, preferred_element_type=F32)
-    return combine(value + jnp.dot(links[:, 256 : 256 + 4 * CDOF], far, preferred_element_type=F32))
+def times_links(links, blocks):
+    field = jnp.concatenate([blocks[0]] + blocks, axis=0)
+    return combine(jnp.dot(links[...], field, preferred_element_type=F32))
 
 
 def send_to_all(me, peers, value, buf, send_sem, recv_sem):
@@ -211,16 +212,12 @@
     op_v,
     col_v,
     rows_v,
-    cells,
     links_v,
     ball_v,
     theta_buf,
     t_buf,
     zx_buf,
     local_sem,
-    halo_send,
-    near_recv,
-    halo_recv,
     sum_send,
     sum_recv,
     peers_in,
@@ -248,14 +245,6 @@
     ball_peers = [
         (lax.rem(t + nt - a, nt), lax.rem(z + nz - b, nz), lax.rem(x + nx - c, nx)) for a, b, c in sites
     ]
-    slots = [
-        (5, (t, lax.rem(z + nz - 1, nz), x)),
-        (6, (t, lax.rem(z + 1, nz), x)),
-        (7, (t, z, lax.rem(x + nx - 1, nx))),
-        (8, (t, z, lax.rem(x + 1, nx))),
-        (3, (lax.rem(t + nt - 1, nt), z, x)),
-        (4, (lax.rem(t + 1, nt), z, x)),
-    ]
     my_t, my_zx = rank_of(t, nt), me_zx
 
     def t_peer(rank):
@@ -272,6 +261,7 @@
             lax.fori_loop(*ranks, step, 0)
 
     barrier = pltpu.get_barrier_semaphore()
+    op_loads[0].start()
     for pair in loads:
         for load in pair:
             load.start()
@@ -281,44 +271,47 @@
     t_peers = [t_peer(k) for k in others(nt, my_t)]
     zx_peers = [zx_peer(k) for k in others(nz * nx, my_zx)]
 
-    for load in op_loads:
+    for load in op_loads[1:]:
         load.start()
     col_load.start()
+
     start = restrict(loads, nv_v, res_v, basis_ref, rows_v)
-    pl.semaphore_wait(barrier, len(sites) - 1 + my_t + my_zx)
-
-    def send_halo(k, wide):
-        own = split(wide)
-        cells[k, 0] = own
-        for m, peer in slots:
+
+    def send_ball(k, wide):
+        ball_v[k, 0] = split(wide)
+        for i in reversed(range(1, len(sites))):
             pltpu.make_async_remote_copy(
-                src_ref=cells.at[k, 0],
-                dst_ref=cells.at[k, m],
-                send_sem=halo_send.at[k],
-                recv_sem=(near_recv if m < 5 else halo_recv).at[k],
-                device_id=peer,
+                src_ref=ball_v.at[k, 0],
+                dst_ref=ball_v.at[k, i],
+                send_sem=ball_send.at[k],
+                recv_sem=ball_recv.at[k],
+                device_id=ball_peers[i],
                 device_id_type=MESH,
             ).start()
-        cells[k, 1] = own
-        cells[k, 2] = own
-
-    def apply_links(k):
-        transfers(cells.at[k, pl.ds(3, 2)], slots[0][1], halo_send.at[k], near_recv.at[k]).wait_recv()
-        near = jnp.dot(
-            links_v[0, :, : 5 * CDOF], cells[k, 0:5].reshape(5 * CDOF, LANES), preferred_element_type=F32
-        )
-        transfers(cells.at[k, pl.ds(5, 4)], slots[0][1], halo_send.at[k], halo_recv.at[k]).wait_recv()
-        far = jnp.dot(
-            links_v[0, :, 256 : 256 + 4 * CDOF], cells[k, 5:9].reshape(4 * CDOF, LANES), preferred_element_type=F32
-        )
-        return combine(near + far)
+
+    def ball_transfers(k):
+        block = ball_v.at[k, pl.ds(1, len(sites) - 1)]
+        return transfers(block, ball_peers[1], ball_send.at[k], ball_recv.at[k])
+
+    def apply_twice(k):
+        ball_transfers(k).wait_recv()
+
+        def block(site, step=(0, 0, 0)):
+            return ball_v[k, sites.index(shifted(site, step, sizes))]
+
+        parts = []
+        for i in range(7):
+            wide = times_links(links_v.at[i], [block(sites[i], step) for step in [(0, 0, 0)] + steps])
+            parts.append(split(wide))
+            if i == 0:
+                once = wide
+        return once, times_links(links_v.at[0], parts)
 
     def sums_of(k, buf, count, peer):
         return transfers(buf.at[pl.ds(0, count - 1)], peer, sum_send.at[k], sum_recv.at[k])
 
-    send_halo(0, both_groups(start))
-    signal_peers(peers_in, (0, my_t), (0, my_zx))
-
+    pl.semaphore_wait(barrier, len(sites) - 1 + my_t + my_zx)
+    send_ball(0, both_groups(start))
     op_loads[0].wait()
     links_v[0] = pack_links(op_v.at[0])
     for i in range(3, 7):
@@ -330,6 +323,7 @@
             device_id=ball_peers[i],
             device_id_type=MESH,
         ).start()
+    signal_peers(peers_in, (0, my_t), (0, my_zx))
 
     col_load.wait()
     eye = lax.broadcasted_iota(jnp.int32, (CDOF, CDOF), 0) == lax.broadcasted_iota(jnp.int32, (CDOF, CDOF), 1)
@@ -349,10 +343,6 @@
         op_loads[i].wait()
         links_v[i] = pack_links(op_v.at[i])
 
-    powers = [start]
-    wide = apply_links(0)
-    send_halo(1, wide)
-    powers.append(first_group(wide))
     answers = nt - 1 - my_t + nz * nx - 1 - my_zx
 
     @pl.when(answers > 0)
@@ -360,18 +350,10 @@
         pl.semaphore_wait(peers_in, answers)
 
     send_to_all(me_zx, zx_peers, stats, theta_buf, sum_send.at[0], sum_recv.at[0])
-    wide = apply_links(1)
-    ball_v[0] = split(wide)
-    for i in reversed(range(1, len(sites))):
-        pltpu.make_async_remote_copy(
-            src_ref=ball_v.at[0],
-            dst_ref=ball_v.at[i],
-            send_sem=ball_send,
-            recv_sem=ball_recv,
-            device_id=ball_peers[i],
-            device_id_type=MESH,
-        ).start()
-    powers.append(first_group(wide))
+    transfers(links_v.at[pl.ds(3, 4)], ball_peers[1], links_send, links_recv).wait_recv()
+    once, twice = apply_twice(0)
+    send_ball(1, twice)
+    powers = [start, first_group(once), first_group(twice)]
 
     sums_of(0, theta_buf, nz * nx, zx_peers[0]).wait_recv()
     stats = jnp.sum(theta_buf[...], axis=0)
@@ -406,23 +388,8 @@
     early += [row_sum(images[0] * images[1]), row_sum(turned[0] * images[1])]
     early = row_of(early, 0)
 
-    transfers(links_v.at[pl.ds(3, 4)], ball_peers[1], links_send, links_recv).wait_recv()
-    transfers(ball_v.at[pl.ds(1, len(sites) - 1)], ball_peers[1], ball_send, ball_recv).wait_recv()
-
-    def block(site, step=(0, 0, 0)):
-        return ball_v[sites.index(shifted(site, step, sizes))]
-
-    parts = []
-    for i in range(7):
-        own = block(sites[i])
-        near = jnp.concatenate([own] * 3 + [block(sites[i], step) for step in steps[:2]], axis=0)
-        far = jnp.concatenate([block(sites[i], step) for step in steps[2:]], axis=0)
-        wide = times_links(links_v[i], near, far)
-        parts.append(split(wide))
-        if i == 0:
-            v3 = first_group(wide) * weights[2]
-    near = jnp.concatenate([parts[0]] * 3 + parts[1:3], axis=0)
-    v4 = first_group(times_links(links_v[0], near, jnp.concatenate(parts[3:], axis=0))) * weights[3]
+    once, twice = apply_twice(1)
+    v3, v4 = first_group(once) * weights[2], first_group(twice) * weights[3]
 
     one.append(v3 - last_one)
     two_next = one[2] - last_two
@@ -475,9 +442,8 @@
     r_ref[...] = remain
 
     transfers(links_v.at[pl.ds(3, 4)], ball_peers[1], links_send, links_recv).wait_send()
-    transfers(ball_v.at[pl.ds(1, len(sites) - 1)], ball_peers[1], ball_send, ball_recv).wait_send()
-    for k in range(2):
-        transfers(cells.at[k, pl.ds(3, 6)], slots[0][1], halo_send.at[k], halo_recv.at[k]).wait_send()
+    ball_transfers(0).wait_send()
+    ball_transfers(1).wait_send()
     sums_of(0, theta_buf, nz * nx, zx_peers[0]).wait_send()
     sums_of(1, t_buf, nt, t_peers[0]).wait_send()
     sums_of(2, zx_buf, nz * nx, zx_peers[0]).wait_send()
@@ -520,23 +486,19 @@
             pltpu.VMEM((3, LINKS, 2, CDOF, CDOF), BF16),
             pltpu.VMEM((nt, 2, CDOF, CDOF), BF16),
             pltpu.VMEM((2 * NVEC * 4, LANES), F32),
-            pltpu.VMEM((2, LINKS, CDOF, LANES), BF16),
-            pltpu.VMEM((7, 2 * CDOF, 512), BF16),
-            pltpu.VMEM((len(ball(sizes)[1]), CDOF, LANES), BF16),
+            pltpu.VMEM((7, 2 * CDOF, 8 * CDOF), BF16),
+            pltpu.VMEM((2, len(ball(sizes)[1]), CDOF, LANES), BF16),
             pltpu.VMEM((nz * nx, 3, LANES), F32),
             pltpu.VMEM((nt, 3, LANES), F32),
             pltpu.VMEM((nz * nx, 3, LANES), F32),
             pltpu.SemaphoreType.DMA((10,)),
-            pltpu.SemaphoreType.DMA((2,)),
-            pltpu.SemaphoreType.DMA((2,)),
-            pltpu.SemaphoreType.DMA((2,)),
             pltpu.SemaphoreType.DMA((3,)),
             pltpu.SemaphoreType.DMA((3,)),
             pltpu.SemaphoreType.REGULAR,
             pltpu.SemaphoreType.DMA,
             pltpu.SemaphoreType.DMA,
-            pltpu.SemaphoreType.DMA,
-            pltpu.SemaphoreType.DMA,
+            pltpu.SemaphoreType.DMA((2,)),
+            pltpu.SemaphoreType.DMA((2,)),
         ],
         compiler_params=pltpu.CompilerParams(
             collective_id=0, has_side_effects=True, vmem_limit_bytes=16 * 1024 * 1024

time: 39.7 us -> 39 us (0.982)
  Pallas kernels: 38.9 us -> 38.3 us
    pallas_call x1, Pallas kernels: 37.7 us -> 37.1 us  [body(): pl.pallas_call(functools.partial(coarse_kernel, sizes), out_shape=(field,...]
where the time goes in v6:
time: 39 us; the launch traced here: 38.9 us
  Pallas kernels  38.3 us (98%)
  between operations  0.64 us (2%)
    pallas_call x1, Pallas kernels, body(): pl.pallas_call(functools.partial(coarse_kernel, sizes), out_shape=(field,...  37.1 us
    pallas_call x1, Pallas kernels, body(): pl.pallas_call(prolong_kernel, out_shape=(jax.ShapeDtypeStruct((2, 4, 3,...  1.2 us

profile of v6, /device:TPU:1, one launch (start us, length us, event | category | flops | bytes accessed | tf_op | source)
XLA Modules:
  0.0 38.9 jit_solution(827982058955463818)
XLA Ops:
  0.6 37.1 %shard_map.50 = (f32[48,128]{1,0:T(8,128)S(1)}, f32[48,128]{1,0:T(8,128)S(1)}, bf16[3,192,512]{2,1,0:T(8,128)(2,1)S(1)}) custom-call(bf16[2,4,3,16,512]{4,3,2,1,0:T(8,128)(2,1)} %bitcast.15, bf16[2,24,3,4,512]{4,3,2,1,0:T(4,128)(2,1)} %bitcast.14, bf16[16,1,1,9,2,48,48]{6,5,4,3,2,1,0:T(8,128)(2,1)} %op_hbm.1), custom_call_target="tpu_custom_call" | custom-call | tf_op jit(solution)/shard_map/pallas_call | solution.py:478
  37.7 1.2 %shard_map.51 = (bf16[2,4,3,16,512]{4,3,2,1,0:T(8,128)(2,1)}, f32[2,16,48]{2,1,0:T(8,128)}) custom-call(f32[48,128]{1,0:T(8,128)S(1)} %get-tuple-element.7.x_ref, f32[48,128]{1,0:T(8,128)S(1)} %get-tuple-element.8.r_ref, bf16[3,192,512]{2,1,0:T(8,128)(2,1)S(1)} %get-tuple-element.9.basis_ref), custom_call_target="tpu_custom_call" | custom-call | tf_op jit(solution)/shard_map/pallas_call | solution.py:507

commit v7 on v6

--- a/solution.py
+++ b/solution.py
@@ -220,7 +220,8 @@
     local_sem,
     sum_send,
     sum_recv,
-    peers_in,
+    t_in,
+    zx_in,
     links_send,
     links_recv,
     ball_send,
@@ -253,12 +254,17 @@
     def zx_peer(rank):
         return t, lax.div(rank, nx), lax.rem(rank, nx)
 
-    def signal_peers(semaphore, t_ranks, zx_ranks):
-        for ranks, peer in ((t_ranks, t_peer), (zx_ranks, zx_peer)):
-            def step(rank, carry, peer=peer):
-                pl.semaphore_signal(semaphore, inc=1, device_id=peer(rank), device_id_type=MESH)
-                return carry
-            lax.fori_loop(*ranks, step, 0)
+    def signal_peers(semaphore, peer, first, count):
+        def step(rank, carry):
+            pl.semaphore_signal(semaphore, inc=1, device_id=peer(rank), device_id_type=MESH)
+            return carry
+
+        lax.fori_loop(first, count, step, 0)
+
+    def wait_peers(semaphore, count):
+        @pl.when(count > 0)
+        def _():
+            pl.semaphore_wait(semaphore, count)
 
     barrier = pltpu.get_barrier_semaphore()
     op_loads[0].start()
@@ -267,7 +273,8 @@
             load.start()
     for peer in ball_peers[1:]:
         pl.semaphore_signal(barrier, inc=1, device_id=peer, device_id_type=MESH)
-    signal_peers(barrier, (my_t + 1, nt), (my_zx + 1, nz * nx))
+    signal_peers(barrier, zx_peer, my_zx + 1, nz * nx)
+    signal_peers(barrier, t_peer, my_t + 1, nt)
     t_peers = [t_peer(k) for k in others(nt, my_t)]
     zx_peers = [zx_peer(k) for k in others(nz * nx, my_zx)]
 
@@ -275,6 +282,8 @@
         load.start()
     col_load.start()
 
+    op_loads[0].wait()
+    links_v[0] = pack_links(op_v.at[0])
     start = restrict(loads, nv_v, res_v, basis_ref, rows_v)
 
     def send_ball(k, wide):
@@ -312,8 +321,6 @@
 
     pl.semaphore_wait(barrier, len(sites) - 1 + my_t + my_zx)
     send_ball(0, both_groups(start))
-    op_loads[0].wait()
-    links_v[0] = pack_links(op_v.at[0])
     for i in range(3, 7):
         pltpu.make_async_remote_copy(
             src_ref=links_v.at[0],
@@ -323,7 +330,7 @@
             device_id=ball_peers[i],
             device_id_type=MESH,
         ).start()
-    signal_peers(peers_in, (0, my_t), (0, my_zx))
+    signal_peers(zx_in, zx_peer, 0, my_zx)
 
     col_load.wait()
     eye = lax.broadcasted_iota(jnp.int32, (CDOF, CDOF), 0) == lax.broadcasted_iota(jnp.int32, (CDOF, CDOF), 1)
@@ -343,16 +350,12 @@
         op_loads[i].wait()
         links_v[i] = pack_links(op_v.at[i])
 
-    answers = nt - 1 - my_t + nz * nx - 1 - my_zx
-
-    @pl.when(answers > 0)
-    def _():
-        pl.semaphore_wait(peers_in, answers)
-
+    wait_peers(zx_in, nz * nx - 1 - my_zx)
     send_to_all(me_zx, zx_peers, stats, theta_buf, sum_send.at[0], sum_recv.at[0])
     transfers(links_v.at[pl.ds(3, 4)], ball_peers[1], links_send, links_recv).wait_recv()
     once, twice = apply_twice(0)
     send_ball(1, twice)
+    signal_peers(t_in, t_peer, 0, my_t)
     powers = [start, first_group(once), first_group(twice)]
 
     sums_of(0, theta_buf, nz * nx, zx_peers[0]).wait_recv()
@@ -406,6 +409,7 @@
     late += [row_sum(turned[i] * images[3]) for i in (0, 1, 2)]
     dense = jnp.concatenate([early, row_of(late[:8], 0), row_of(late[8:], 0)], axis=0)
 
+    wait_peers(t_in, nt - 1 - my_t)
     send_to_all(t, t_peers, dense, t_buf, sum_send.at[1], sum_recv.at[1])
     turned.append(times_i(images[3]))
     basis_turned = [times_i(field) for field in basis]
@@ -495,6 +499,7 @@
             pltpu.SemaphoreType.DMA((3,)),
             pltpu.SemaphoreType.DMA((3,)),
             pltpu.SemaphoreType.REGULAR,
+            pltpu.SemaphoreType.REGULAR,
             pltpu.SemaphoreType.DMA,
             pltpu.SemaphoreType.DMA,
             pltpu.SemaphoreType.DMA((2,)),

time: 39 us -> 38.6 us (0.990)
  Pallas kernels: 38.3 us -> 37.9 us
where the time goes in v7:
time: 38.6 us; the launch traced here: 38.5 us
  Pallas kernels  37.9 us (98%)
  between operations  0.64 us (2%)
    pallas_call x1, Pallas kernels, body(): pl.pallas_call(functools.partial(coarse_kernel, sizes), out_shape=(field,...  36.7 us
    pallas_call x1, Pallas kernels, body(): pl.pallas_call(prolong_kernel, out_shape=(jax.ShapeDtypeStruct((2, 4, 3,...  1.21 us

profile of v7, /device:TPU:1, one launch (start us, length us, event | category | flops | bytes accessed | tf_op | source)
XLA Modules:
  0.0 38.5 jit_solution(12321533724997485041)
XLA Ops:
  0.6 36.7 %shard_map.50 = (f32[48,128]{1,0:T(8,128)S(1)}, f32[48,128]{1,0:T(8,128)S(1)}, bf16[3,192,512]{2,1,0:T(8,128)(2,1)S(1)}) custom-call(bf16[2,4,3,16,512]{4,3,2,1,0:T(8,128)(2,1)} %bitcast.15, bf16[2,24,3,4,512]{4,3,2,1,0:T(4,128)(2,1)} %bitcast.14, bf16[16,1,1,9,2,48,48]{6,5,4,3,2,1,0:T(8,128)(2,1)} %op_hbm.1), custom_call_target="tpu_custom_call" | custom-call | tf_op jit(solution)/shard_map/pallas_call | solution.py:482
  37.3 1.2 %shard_map.51 = (bf16[2,4,3,16,512]{4,3,2,1,0:T(8,128)(2,1)}, f32[2,16,48]{2,1,0:T(8,128)}) custom-call(f32[48,128]{1,0:T(8,128)S(1)} %get-tuple-element.7.x_ref, f32[48,128]{1,0:T(8,128)S(1)} %get-tuple-element.8.r_ref, bf16[3,192,512]{2,1,0:T(8,128)(2,1)S(1)} %get-tuple-element.9.basis_ref), custom_call_target="tpu_custom_call" | custom-call | tf_op jit(solution)/shard_map/pallas_call | solution.py:512

commit v8 on v7

--- a/solution.py
+++ b/solution.py
@@ -344,7 +344,8 @@
     scale = 1.0 / (nt * nz * nx * CDOF)
     stats = [jnp.where(eye, trace[0], 0.0), jnp.where(eye, trace[1], 0.0), square]
     stats = [jnp.sum(row_sum(value), axis=1, keepdims=True) * scale for value in stats]
-    stats = jnp.concatenate([jnp.broadcast_to(value, (1, LANES)) for value in stats], axis=0)
+    place = lane_iota((1, LANES))
+    stats = sum(jnp.where(place == i, value, 0.0) for i, value in enumerate(stats))
 
     for i in (1, 2):
         op_loads[i].wait()
@@ -360,9 +361,13 @@
 
     sums_of(0, theta_buf, nz * nx, zx_peers[0]).wait_recv()
     stats = jnp.sum(theta_buf[...], axis=0)
-    square = stats[2:3]
+    stats = [
+        jnp.broadcast_to(jnp.sum(jnp.where(place == i, stats, 0.0), axis=1, keepdims=True), (1, LANES))
+        for i in range(3)
+    ]
+    square = stats[2]
     inverse = jnp.where(square > 0.0, lax.rsqrt(jnp.where(square > 0.0, square, 1.0)), 1.0)
-    theta = (stats[0:1] * inverse, stats[1:2] * inverse)
+    theta = (stats[0] * inverse, stats[1] * inverse)
     weights = [inverse]
     for _ in range(3):
         weights.append(weights[-1] * inverse)
@@ -492,7 +497,7 @@
             pltpu.VMEM((2 * NVEC * 4, LANES), F32),
             pltpu.VMEM((7, 2 * CDOF, 8 * CDOF), BF16),
             pltpu.VMEM((2, len(ball(sizes)[1]), CDOF, LANES), BF16),
-            pltpu.VMEM((nz * nx, 3, LANES), F32),
+            pltpu.VMEM((nz * nx, 1, LANES), F32),
             pltpu.VMEM((nt, 3, LANES), F32),
             pltpu.VMEM((nz * nx, 3, LANES), F32),
             pltpu.SemaphoreType.DMA((10,)),

time: 38.6 us -> 38.3 us (level)
  Pallas kernels: 37.9 us -> 37.5 us
where the time goes in v8:
time: 38.3 us; the launch traced here: 38.2 us
  Pallas kernels  37.5 us (98%)
  between operations  0.64 us (2%)
    pallas_call x1, Pallas kernels, body(): pl.pallas_call(functools.partial(coarse_kernel, sizes), out_shape=(field,...  36.3 us
    pallas_call x1, Pallas kernels, body(): pl.pallas_call(prolong_kernel, out_shape=(jax.ShapeDtypeStruct((2, 4, 3,...  1.21 us

profile of v8, /device:TPU:1, one launch (start us, length us, event | category | flops | bytes accessed | tf_op | source)
XLA Modules:
  0.0 38.2 jit_solution(15621713696572260393)
XLA Ops:
  0.6 36.3 %shard_map.50 = (f32[48,128]{1,0:T(8,128)S(1)}, f32[48,128]{1,0:T(8,128)S(1)}, bf16[3,192,512]{2,1,0:T(8,128)(2,1)S(1)}) custom-call(bf16[2,4,3,16,512]{4,3,2,1,0:T(8,128)(2,1)} %bitcast.15, bf16[2,24,3,4,512]{4,3,2,1,0:T(4,128)(2,1)} %bitcast.14, bf16[16,1,1,9,2,48,48]{6,5,4,3,2,1,0:T(8,128)(2,1)} %op_hbm.1), custom_call_target="tpu_custom_call" | custom-call | tf_op jit(solution)/shard_map/pallas_call | solution.py:487
  37.0 1.2 %shard_map.51 = (bf16[2,4,3,16,512]{4,3,2,1,0:T(8,128)(2,1)}, f32[2,16,48]{2,1,0:T(8,128)}) custom-call(f32[48,128]{1,0:T(8,128)S(1)} %get-tuple-element.7.x_ref, f32[48,128]{1,0:T(8,128)S(1)} %get-tuple-element.8.r_ref, bf16[3,192,512]{2,1,0:T(8,128)(2,1)S(1)} %get-tuple-element.9.basis_ref), custom_call_target="tpu_custom_call" | custom-call | tf_op jit(solution)/shard_map/pallas_call | solution.py:517

commit v9 on v8

--- a/solution.py
+++ b/solution.py
@@ -278,9 +278,6 @@
     t_peers = [t_peer(k) for k in others(nt, my_t)]
     zx_peers = [zx_peer(k) for k in others(nz * nx, my_zx)]
 
-    for load in op_loads[1:]:
-        load.start()
-    col_load.start()
 
     op_loads[0].wait()
     links_v[0] = pack_links(op_v.at[0])
@@ -320,6 +317,9 @@
         return transfers(buf.at[pl.ds(0, count - 1)], peer, sum_send.at[k], sum_recv.at[k])
 
     pl.semaphore_wait(barrier, len(sites) - 1 + my_t + my_zx)
+    col_load.start()
+    for load in op_loads[1:]:
+        load.start()
     send_ball(0, both_groups(start))
     for i in range(3, 7):
         pltpu.make_async_remote_copy(

time: 38.3 us -> 38.3 us (level)
  no operation moved by 1% of the time
where the time goes in v9:
time: 38.3 us; the launch traced here: 38.2 us
  Pallas kernels  37.5 us (98%)
  between operations  0.64 us (2%)
    pallas_call x1, Pallas kernels, body(): pl.pallas_call(functools.partial(coarse_kernel, sizes), out_shape=(field,...  36.3 us
    pallas_call x1, Pallas kernels, body(): pl.pallas_call(prolong_kernel, out_shape=(jax.ShapeDtypeStruct((2, 4, 3,...  1.21 us

profile of v9, /device:TPU:1, one launch (start us, length us, event | category | flops | bytes accessed | tf_op | source)
XLA Modules:
  0.0 38.2 jit_solution(5008772059118988057)
XLA Ops:
  0.6 36.3 %shard_map.50 = (f32[48,128]{1,0:T(8,128)S(1)}, f32[48,128]{1,0:T(8,128)S(1)}, bf16[3,192,512]{2,1,0:T(8,128)(2,1)S(1)}) custom-call(bf16[2,4,3,16,512]{4,3,2,1,0:T(8,128)(2,1)} %bitcast.15, bf16[2,24,3,4,512]{4,3,2,1,0:T(4,128)(2,1)} %bitcast.14, bf16[16,1,1,9,2,48,48]{6,5,4,3,2,1,0:T(8,128)(2,1)} %op_hbm.1), custom_call_target="tpu_custom_call" | custom-call | tf_op jit(solution)/shard_map/pallas_call | solution.py:487
  37.0 1.2 %shard_map.51 = (bf16[2,4,3,16,512]{4,3,2,1,0:T(8,128)(2,1)}, f32[2,16,48]{2,1,0:T(8,128)}) custom-call(f32[48,128]{1,0:T(8,128)S(1)} %get-tuple-element.7.x_ref, f32[48,128]{1,0:T(8,128)S(1)} %get-tuple-element.8.r_ref, bf16[3,192,512]{2,1,0:T(8,128)(2,1)S(1)} %get-tuple-element.9.basis_ref), custom_call_target="tpu_custom_call" | custom-call | tf_op jit(solution)/shard_map/pallas_call | solution.py:517
